TPU v7x, 128 devices: a whole 4x4x4 slice. The times are simulated.
128 devices in a mesh: tm: 8 (over z_lo, y), space: 16 (over x, z_hi, core).
Axes of the slice: x: 4, y: 4, z: 4 (z_hi: 2, z_lo: 2; z = z_hi * 2 + z_lo), core: 2. Of those that a mesh axis runs over, the one named last changes fastest.
Arguments:
- start: float32 [16, 3, 8, 64, 1024], P(None, None, 'tm', 'space'), may hold values from -400 to 400
- smear_links: float32 [3, 3, 3, 8, 64, 1024], P(None, None, None, 'tm', 'space'), may hold values from -1 to 1, as said below
- fat_links: float32 [4, 3, 3, 8, 64, 1024], P(None, None, None, 'tm', 'space'), may hold values from -1 to 1, as said below
- naik_links: float32 [4, 3, 3, 8, 64, 1024], P(None, None, None, 'tm', 'space'), may hold values from -1 to 1, as said below
Outputs:
- projected: float32 [8, 16, 16], P('tm')
- solution: float32 [16, 3, 64, 64, 128], P(None, None, 'space', 'tm')
Inputs may be any that keep to these rules, and one draw needn't show every extreme that they name: `smear_links`: every link is a real orthogonal 3 x 3 matrix of determinant one. `fat_links`: every link is a real orthogonal 3 x 3 matrix of determinant one. `naik_links`: every link is a real orthogonal 3 x 3 matrix of determinant one.
All inputs are finite; a program needn't handle non-finite values.
Results may differ from a plain program's by a relative error of at most 0.0003.
Values sent between devices are 32-bit elements; how exact they have to be, the bound alone decides.
A program may use at most 128 MiB of HBM per device.

v0:
```python
import jax
import jax.numpy as jnp
from jax import lax
from jax.sharding import PartitionSpec as P

Z = 16
CHEB = 3
ITERS = 2


HIGH = lax.Precision.HIGHEST
CENTER = 6.5
HALF_WIDTH = 5.5
MASS = 0.5
ONE_HOP = 1.125
THREE_HOP = -1.0 / 24.0


def extended_2(cells, sides, width):
    for axis, dim in sides:
        count = lax.axis_size(axis)
        head = lax.slice_in_dim(cells, 0, width, axis=dim)
        tail = lax.slice_in_dim(cells, cells.shape[dim] - width, cells.shape[dim], axis=dim)
        cells = jnp.concatenate(
            [
                lax.ppermute(tail, axis, [(i, (i + 1) % count) for i in range(count)]),
                cells,
                lax.ppermute(head, axis, [((i + 1) % count, i) for i in range(count)]),
            ],
            axis=dim,
        )
    return cells


def from_behind(value, axis, steps):
    count = lax.axis_size(axis)
    leading, last = (max(0, -steps), min(count, count - steps))
    return lax.ppermute(value, axis, [(source, source + steps) for source in range(leading, last)])


def turn(links, field):
    return jnp.stack(
        [
            links[a, 0] * field[:, 0] + links[a, 1] * field[:, 1] + links[a, 2] * field[:, 2]
            for a in range(3)
        ],
        axis=1,
    )


def turn_back(links, field):
    return jnp.stack(
        [
            links[0, a] * field[:, 0] + links[1, a] * field[:, 1] + links[2, a] * field[:, 2]
            for a in range(3)
        ],
        axis=1,
    )


def shift_z(field, step, zlen):
    length = field.shape[-1]
    zpos = jnp.arange(length) % zlen
    ahead = jnp.roll(field, -step, axis=-1)
    if step > 0:
        return jnp.where(zpos + step < zlen, ahead, jnp.roll(field, zlen - step, axis=-1))
    return jnp.where(zpos + step >= 0, ahead, jnp.roll(field, -step - zlen, axis=-1))


def alternate(values, shape):
    return jnp.broadcast_to(1 - 2 * (values % 2), shape).astype(jnp.float32)


def geometry(tpos, xpos, ypos, zpos, shape):
    signs = [
        jnp.ones(shape, jnp.float32),
        alternate(xpos, shape),
        alternate(xpos + ypos, shape),
        alternate(xpos + ypos + zpos, shape),
    ]
    even = ((tpos + xpos + ypos + zpos) % 2 == 0).astype(jnp.float32)
    return (signs, even)


def lower_inverse(gram):
    lower = jnp.linalg.cholesky(gram)
    ident = jnp.broadcast_to(jnp.eye(gram.shape[-1], dtype=jnp.float32), gram.shape)
    return lax.linalg.triangular_solve(lower, ident, left_side=True, lower=True)


def slab_halo(field):
    return extended_2(field, (("space", 3),), 1)


def deep_halo(field):
    return extended_2(field, (("space", 3),), 3)


def time_shift(field, step):
    return from_behind(field, "tm", step)


def space_sum(values):
    return lax.psum(values, "space")


def lattice_sum(values):
    return lax.psum(values, ("tm", "space"))


def slab_laplace(field, links, rim_links, zlen):
    extended = slab_halo(field)
    planes = field.shape[3]
    total = 6.0 * field
    total = total - (
        turn(links[0], extended[:, :, :, 2:, :])
        + turn_back(rim_links[:, :, :, :planes, :], extended[:, :, :, :planes, :])
    )
    total = total - (
        turn(links[1], jnp.roll(field, -zlen, axis=4))
        + jnp.roll(turn_back(links[1], field), zlen, axis=4)
    )
    total = total - (
        turn(links[2], shift_z(field, 1, zlen)) + shift_z(turn_back(links[2], field), -1, zlen)
    )
    return total


def slab_hop(field, fat, naik, rims, signs, zlen):
    extended = deep_halo(field)
    planes = field.shape[3]
    total = jnp.zeros_like(field)
    for mu in range(4):
        for links, rim, depth, weight in (
            (fat, rims[0], 1, ONE_HOP),
            (naik, rims[1], 3, THREE_HOP),
        ):
            if mu == 0:
                ahead = extended[:, :, :, 3 + depth : 3 + depth + planes, :]
                behind = turn_back(
                    rim[:, :, :, 3 - depth : 3 - depth + planes, :],
                    extended[:, :, :, 3 - depth : 3 - depth + planes, :],
                )
            elif mu == 1:
                ahead = jnp.roll(field, -depth * zlen, axis=4)
                behind = jnp.roll(turn_back(links[mu], field), depth * zlen, axis=4)
            elif mu == 2:
                ahead = shift_z(field, depth, zlen)
                behind = shift_z(turn_back(links[mu], field), -depth, zlen)
            else:
                ahead = time_shift(field, -depth)
                behind = time_shift(turn_back(links[mu], field), depth)
            total = total + weight * signs[mu] * (turn(links[mu], ahead) - behind)
    return 0.5 * total


def to_block_order(field, zlen):
    comps, tloc, planes, cells = field.shape
    rows = cells // zlen
    return (
        field.reshape(comps, tloc, planes, rows, zlen)
        .transpose(0, 2, 3, 1, 4)
        .reshape(comps, planes, rows, tloc * zlen)
    )


def inner(left, right):
    return jnp.sum(left * right, axis=(1, 2, 3, 4))


def spread(values):
    return values[:, None, None, None, None]


def conjugate(rhs, normal):
    solution = jnp.zeros_like(rhs)
    resid = rhs
    direc = rhs
    norm_now = lattice_sum(inner(resid, resid))
    for step in range(ITERS):
        image = normal(direc)
        alpha = norm_now / lattice_sum(inner(direc, image))
        solution = solution + spread(alpha) * direc
        if step + 1 < ITERS:
            resid = resid - spread(alpha) * image
            norm_next = lattice_sum(inner(resid, resid))
            direc = resid + spread(norm_next / norm_now) * direc
            norm_now = norm_next
    return solution


def body(start, smear_links, fat_links, naik_links):
    zlen = Z
    nvec, tloc, planes, cells = (start.shape[0], start.shape[2], start.shape[3], start.shape[4])
    comps = nvec * 3
    count = 3.0 * (planes * lax.axis_size("space")) * cells
    rim_links = slab_halo(smear_links[0])

    def sigma(field):
        return (slab_laplace(field, smear_links, rim_links, zlen) - CENTER * field) / HALF_WIDTH

    earlier = start
    current = sigma(start)
    for step in range(CHEB - 1):
        earlier, current = (current, 2.0 * sigma(current) - earlier)
    gram_part = jnp.einsum("kctxs,jctxs->tkj", current, current, precision=HIGH)
    inverse = lower_inverse(space_sum(gram_part) / count)
    basis = jnp.einsum("tkj,jctxs->kctxs", inverse, current, precision=HIGH)
    image = slab_laplace(basis, smear_links, rim_links, zlen)
    projected = space_sum(jnp.einsum("kctxs,jctxs->tkj", basis, image, precision=HIGH)) / count
    rim_both = deep_halo(jnp.concatenate([fat_links[0], naik_links[0]], axis=0))
    rims = (rim_both[:3], rim_both[3:])
    tpos = (lax.axis_index("tm") * tloc + jnp.arange(tloc))[:, None, None]
    xpos = (lax.axis_index("space") * planes + jnp.arange(planes))[None, :, None]
    places = jnp.arange(cells)[None, None, :]
    signs, even = geometry(tpos, xpos, places // zlen, places % zlen, (tloc, planes, cells))

    def normal(field):
        return MASS * MASS * field - slab_hop(
            slab_hop(field, fat_links, naik_links, rims, signs, zlen),
            fat_links,
            naik_links,
            rims,
            signs,
            zlen,
        )

    slab_solution = conjugate(basis * even, normal)
    moved = lax.all_to_all(
        slab_solution.reshape(comps, tloc, planes, cells),
        "tm",
        split_axis=3,
        concat_axis=1,
        tiled=True,
    )
    blocked = to_block_order(moved, zlen)
    solution = blocked.reshape((nvec, 3) + blocked.shape[1:])
    return (projected, solution)


def solution(mesh):
    in_specs = (
        P(None, None, "tm", "space", None),
        P(None, None, None, "tm", "space", None),
        P(None, None, None, "tm", "space", None),
        P(None, None, None, "tm", "space", None),
    )
    out_specs = (P("tm", None, None), P(None, None, "space", "tm", None))
    return jax.shard_map(body, mesh=mesh, in_specs=in_specs, out_specs=out_specs, check_vma=False)
```

profile of v0, /device:TPU:0, one launch (start us, length us, event | category | flops | bytes accessed | tf_op | source)
XLA Modules:
  0.0 690.5 jit_solution(14905407970242637657)
XLA Ops:
  0.6 1.9 slice_bitcast_fusion.10
  4.4 4.1 collective-permute-start.2
  8.5 1.5 collective-permute-start
  39.7 5.4 collective-permute-start.3
  46.9 1.5 fusion.272
  48.4 1.5 maximum_bitcast_fusion.16
  49.9 3.9 collective-permute-done.4
  57.7 5.4 collective-permute-start.5
  63.2 2.5 collective-permute-done.6
  69.0 39.1 %psum.42 = f32[1,16,16]{1,2,0:T(8,128)S(1)} all-reduce(f32[1,16,16]{1,2,0:T(8,128)S(1)} %convolution_bitcast_fusion.1), channel_id=1, replica_groups=mesh['tm'=8,'space'=16] {'space'}, use_global_device_ids=true, to_apply=%region_0.1 | all-reduce | flops 256 | bytes 2048 | tf_op jit(solution)/shard_map/psum | solution.py:104
  130.0 5.3 collective-permute-start.7
  138.6 6.8 collective-permute-start.15
  145.5 5.3 collective-permute-start.9
  152.0 5.6 collective-permute-start.13
  158.4 4.8 collective-permute-done.9
  164.1 5.1 collective-permute-done.13
  169.3 2.3 fusion.79
  176.3 3.7 collective-permute-start.16
  181.5 4.7 collective-permute-start.19
  187.4 24.7 %collective-permute-start.21 = (f32[16,3,1,4,1024]{4,0,3,1,2:T(8,128)S(1)}, f32[16,3,1,4,1024]{4,0,3,1,2:T(8,128)S(1)}, u32[]{:S(2)}, u32[]{:S(2)}) collective-permute-start(f32[16,3,1,4,1024]{4,0,3,1,2:T(8,128)S(1)} %pad_maximum_fusion.112), channel_id=1, source_target_pairs={{0,48},{16,64},{32,80},{48,96},{64,112},{1,49},{17,65},{33,81},{49... | collective-permute-start | bytes 2359304 | tf_op jit(solution)/shard_map/ppermute | solution.py:38
  215.4 12.6 %collective-permute-done.21 = f32[16,3,1,4,1024]{4,0,3,1,2:T(8,128)S(1)} collective-permute-done((f32[16,3,1,4,1024]{4,0,3,1,2:T(8,128)S(1)}, f32[16,3,1,4,1024]{4,0,3,1,2:T(8,128)S(1)}, u32[]{:S(2)}, u32[]{:S(2)}) %collective-permute-start.21) | collective-permute-done | bytes 786464 | tf_op jit(solution)/shard_map/ppermute | solution.py:38
  228.0 3.0 multiply_reduce_fusion.1
  231.0 96.2 %all-reduce = (f32[16]{0:T(128)}, f32[16]{0:T(128)}) all-reduce(f32[16]{0:T(128)} %get-tuple-element.13, f32[16]{0:T(128)} %get-tuple-element.12), channel_id=1, replica_groups=mesh['tm'=8,'space'=16] {'tm','space'}, use_global_device_ids=true, to_apply=%region_5.6 | all-reduce | flops 32 | bytes 256 | tf_op jit(solution)/shard_map/psum | solution.py:108
  330.1 62.0 %psum.46 = f32[16]{0:T(128)S(1)} all-reduce(f32[16]{0:T(128)} %multiply_reduce_fusion), channel_id=1, replica_groups=mesh['tm'=8,'space'=16] {'tm','space'}, use_global_device_ids=true, to_apply=%region_9.10 | all-reduce | flops 16 | bytes 128 | tf_op jit(solution)/shard_map/psum | solution.py:108
  400.6 6.4 collective-permute-start.27
  409.1 5.3 collective-permute-start.22
  415.2 8.0 %collective-permute-done.23 = f32[16,3,1,3,1024]{4,0,3,1,2:T(8,128)S(1)} collective-permute-done((f32[16,3,1,3,1024]{4,0,3,1,2:T(8,128)S(1)}, f32[16,3,1,3,1024]{4,0,3,1,2:T(8,128)S(1)}, u32[]{:S(2)}, u32[]{:S(2)}) %collective-permute-start.23) | collective-permute-done | bytes 589856 | tf_op jit(solution)/shard_map/ppermute | solution.py:26
  423.1 6.3 collective-permute-start.25
  431.5 7.1 %collective-permute-done.25 = f32[16,3,1,4,1024]{4,0,3,1,2:T(8,128)S(1)} collective-permute-done((f32[16,3,1,4,1024]{4,0,3,1,2:T(8,128)S(1)}, f32[16,3,1,4,1024]{4,0,3,1,2:T(8,128)S(1)}, u32[]{:S(2)}, u32[]{:S(2)}) %collective-permute-start.25) | collective-permute-done | bytes 786464 | tf_op jit(solution)/shard_map/ppermute | solution.py:38
  438.7 2.4 fusion.32
  445.9 35.7 %collective-permute-start.29 = (f32[16,3,1,3,1024]{4,0,3,1,2:T(8,128)S(1)}, f32[16,3,1,3,1024]{4,0,3,1,2:T(8,128)S(1)}, u32[]{:S(2)}, u32[]{:S(2)}) collective-permute-start(f32[16,3,1,3,1024]{4,0,3,1,2:T(8,128)S(1)} %get-tuple-element.157), channel_id=1, source_target_pairs={{0,1},{1,2},{2,3},{3,4},{4,5},{5,6},{6,7},{7,8},{8,9},{9,10},{10,1... | collective-permute-start | bytes 1769480 | tf_op jit(solution)/shard_map/ppermute | solution.py:26
  482.8 5.2 collective-permute-start.31
  489.2 6.8 collective-permute-start.33
  497.8 4.4 collective-permute-done.31
  502.3 3.2 collective-permute-done.33
  505.5 3.1 fusion.191
  509.6 103.6 %psum.47 = f32[16]{0:T(128)S(1)} all-reduce(f32[16]{0:T(128)} %fusion.191), channel_id=1, replica_groups=mesh['tm'=8,'space'=16] {'tm','space'}, use_global_device_ids=true, to_apply=%region_11.12 | all-reduce | flops 16 | bytes 128 | tf_op jit(solution)/shard_map/psum | solution.py:108
  615.1 1.8 copy.122
  617.0 4.6 reshape.7396
  621.6 3.7 all-to-all-start
  626.6 3.1 convolution_bitcast_fusion
  629.8 35.6 %psum.43 = f32[1,16,16]{1,2,0:T(8,128)S(1)} all-reduce(f32[1,16,16]{1,2,0:T(8,128)S(1)} %convolution_bitcast_fusion), channel_id=1, replica_groups=mesh['tm'=8,'space'=16] {'space'}, use_global_device_ids=true, to_apply=%region_3.4 | all-reduce | flops 256 | bytes 2048 | tf_op jit(solution)/shard_map/psum | solution.py:104
  666.5 2.5 reduce.9
  669.0 3.6 reshape.7397
  672.6 2.8 copy.123
  675.5 2.0 copy.124
  677.5 7.4 %copy.125 = f32[48,4,8,8,16]{4,3,2,1,0:T(8,128)} copy(f32[48,4,8,8,16]{0,4,2,1,3:T(8,128)} %bitcast.375) | data formatting | bytes 1572864 | tf_op jit(solution)/shard_map/transpose | solution.py:162
  684.9 5.1 reshape_reshape.3
  (906 shorter events, 105.6 us)
Async XLA Ops:
  3.2 28.2 %collective-permute-start.1 = (f32[3,3,1,1,1024]{4,3,1,0,2:T(1,128)}, f32[3,3,1,1,1024]{4,3,1,0,2:T(1,128)}, u32[]{:S(2)}, u32[]{:S(2)}) collective-permute-start(f32[3,3,1,1,1024]{4,3,1,0,2:T(1,128)} %slice.3515), channel_id=1, source_target_pairs={{0,1},{1,2},{2,3},{3,4},{4,5},{5,6},{6,7},{7,8},{8,9},{9,10},{10,1... | collective-permute-start | bytes 110600 | tf_op jit(solution)/shard_map/ppermute | solution.py:26
  4.4 27.9 %collective-permute-start.2 = (f32[16,3,1,1,1024]{4,0,3,1,2:T(8,128)}, f32[16,3,1,1,1024]{4,0,3,1,2:T(8,128)}, u32[]{:S(2)}, u32[]{:S(2)}) collective-permute-start(f32[16,3,1,1,1024]{4,0,3,1,2:T(8,128)} %get-tuple-element.334), channel_id=1, source_target_pairs={{0,1},{1,2},{2,3},{3,4},{4,5},{5,6},{6,7},{7,8},{8,9},{9,10},{10,1... | collective-permute-start | bytes 589832 | tf_op jit(solution)/shard_map/ppermute | solution.py:26
  8.5 25.5 %collective-permute-start = (f32[16,3,1,1,1024]{4,0,3,1,2:T(8,128)}, f32[16,3,1,1,1024]{4,0,3,1,2:T(8,128)}, u32[]{:S(2)}, u32[]{:S(2)}) collective-permute-start(f32[16,3,1,1,1024]{4,0,3,1,2:T(8,128)} %get-tuple-element.333), channel_id=1, source_target_pairs={{1,0},{2,1},{3,2},{4,3},{5,4},{6,5},{7,6},{8,7},{9,8},{10,9},{11,1... | collective-permute-start | bytes 589832 | tf_op jit(solution)/shard_map/ppermute | solution.py:28
  11.7 33.8 %collective-permute-start.10 = (f32[6,3,1,3,1024]{4,3,1,0,2:T(4,128)}, f32[6,3,1,3,1024]{4,3,1,0,2:T(4,128)}, u32[]{:S(2)}, u32[]{:S(2)}) collective-permute-start(f32[6,3,1,3,1024]{4,3,1,0,2:T(4,128)} %pad_maximum_fusion.121), channel_id=1, source_target_pairs={{0,1},{1,2},{2,3},{3,4},{4,5},{5,6},{6,7},{7,8},{8,9},{9,10},{10,1... | collective-permute-start | bytes 663560 | tf_op jit(solution)/shard_map/ppermute | solution.py:26
  32.2 33.5 %copy-start.258 = (f32[4,1024]{1,0:T(4,128)}, f32[4,1024]{1,0:T(4,128)S(1)}, u32[]{:S(2)}) copy-start(f32[4,1024]{1,0:T(4,128)S(1)} %get-tuple-element.374) | copy-start | bytes 49156
  32.2 33.9 %copy-start.242 = (f32[4,1024]{1,0:T(4,128)}, f32[4,1024]{1,0:T(4,128)S(1)}, u32[]{:S(2)}) copy-start(f32[4,1024]{1,0:T(4,128)S(1)} %get-tuple-element.375) | copy-start | bytes 49156
  32.2 33.9 %copy-start.244 = (f32[4,1024]{1,0:T(4,128)}, f32[4,1024]{1,0:T(4,128)S(1)}, u32[]{:S(2)}) copy-start(f32[4,1024]{1,0:T(4,128)S(1)} %get-tuple-element.376) | copy-start | bytes 49156
  32.2 33.9 %copy-start.246 = (f32[4,1024]{1,0:T(4,128)}, f32[4,1024]{1,0:T(4,128)S(1)}, u32[]{:S(2)}) copy-start(f32[4,1024]{1,0:T(4,128)S(1)} %get-tuple-element.377) | copy-start | bytes 49156
  32.3 33.9 %copy-start.248 = (f32[4,1024]{1,0:T(4,128)}, f32[4,1024]{1,0:T(4,128)S(1)}, u32[]{:S(2)}) copy-start(f32[4,1024]{1,0:T(4,128)S(1)} %get-tuple-element.378) | copy-start | bytes 49156
  32.3 33.9 %copy-start.250 = (f32[4,1024]{1,0:T(4,128)}, f32[4,1024]{1,0:T(4,128)S(1)}, u32[]{:S(2)}) copy-start(f32[4,1024]{1,0:T(4,128)S(1)} %get-tuple-element.379) | copy-start | bytes 49156
  32.3 33.9 %copy-start.252 = (f32[4,1024]{1,0:T(4,128)}, f32[4,1024]{1,0:T(4,128)S(1)}, u32[]{:S(2)}) copy-start(f32[4,1024]{1,0:T(4,128)S(1)} %get-tuple-element.382) | copy-start | bytes 49156
  32.3 34.1 %copy-start.264 = (f32[4,1024]{1,0:T(4,128)}, f32[4,1024]{1,0:T(4,128)S(1)}, u32[]{:S(2)}) copy-start(f32[4,1024]{1,0:T(4,128)S(1)} %get-tuple-element.455) | copy-start | bytes 49156
  39.7 10.2 %collective-permute-start.3 = (f32[16,3,1,1,1024]{4,0,3,1,2:T(8,128)S(1)}, f32[16,3,1,1,1024]{4,0,3,1,2:T(8,128)S(1)}, u32[]{:S(2)}, u32[]{:S(2)}) collective-permute-start(f32[16,3,1,1,1024]{4,0,3,1,2:T(8,128)S(1)} %get-tuple-element.324), channel_id=1, source_target_pairs={{1,0},{2,1},{3,2},{4,3},{5,4},{6,5},{7,6},{8,7},{9,8},{10,9},{11,1... | collective-permute-start | bytes 589832 | tf_op jit(solution)/shard_map/ppermute | solution.py:28
  45.2 8.7 %collective-permute-start.4 = (f32[16,3,1,1,1024]{4,0,3,1,2:T(8,128)S(1)}, f32[16,3,1,1,1024]{4,0,3,1,2:T(8,128)S(1)}, u32[]{:S(2)}, u32[]{:S(2)}) collective-permute-start(f32[16,3,1,1,1024]{4,0,3,1,2:T(8,128)S(1)} %get-tuple-element.323), channel_id=1, source_target_pairs={{0,1},{1,2},{2,3},{3,4},{4,5},{5,6},{6,7},{7,8},{8,9},{9,10},{10,1... | collective-permute-start | bytes 589832 | tf_op jit(solution)/shard_map/ppermute | solution.py:26
  46.9 116.5 %copy-start.199 = (f32[4,1024]{1,0:T(4,128)}, f32[4,1024]{1,0:T(4,128)S(1)}, u32[]{:S(2)}) copy-start(f32[4,1024]{1,0:T(4,128)S(1)} %get-tuple-element.401) | copy-start | bytes 49156
  48.4 109.6 %copy-start.202 = (f32[4,1024]{1,0:T(4,128)}, f32[4,1024]{1,0:T(4,128)S(1)}, u32[]{:S(2)}) copy-start(f32[4,1024]{1,0:T(4,128)S(1)} %get-tuple-element.358) | copy-start | bytes 49156
  48.4 109.6 %copy-start.205 = (f32[4,1024]{1,0:T(4,128)}, f32[4,1024]{1,0:T(4,128)S(1)}, u32[]{:S(2)}) copy-start(f32[4,1024]{1,0:T(4,128)S(1)} %get-tuple-element.359) | copy-start | bytes 49156
  49.9 113.5 %copy-start.196 = (f32[4,1024]{1,0:T(4,128)}, f32[4,1024]{1,0:T(4,128)S(1)}, u32[]{:S(2)}) copy-start(f32[4,1024]{1,0:T(4,128)S(1)} %get-tuple-element.403) | copy-start | bytes 49156
  56.7 9.0 %collective-permute-start.6 = (f32[16,3,1,1,1024]{4,0,3,1,2:T(8,128)S(1)}, f32[16,3,1,1,1024]{4,0,3,1,2:T(8,128)S(1)}, u32[]{:S(2)}, u32[]{:S(2)}) collective-permute-start(f32[16,3,1,1,1024]{4,0,3,1,2:T(8,128)S(1)} %get-tuple-element.306), channel_id=1, source_target_pairs={{0,1},{1,2},{2,3},{3,4},{4,5},{5,6},{6,7},{7,8},{8,9},{9,10},{10,1... | collective-permute-start | bytes 589832 | tf_op jit(solution)/shard_map/ppermute | solution.py:26
  57.7 8.7 %collective-permute-start.5 = (f32[16,3,1,1,1024]{4,0,3,1,2:T(8,128)S(1)}, f32[16,3,1,1,1024]{4,0,3,1,2:T(8,128)S(1)}, u32[]{:S(2)}, u32[]{:S(2)}) collective-permute-start(f32[16,3,1,1,1024]{4,0,3,1,2:T(8,128)S(1)} %get-tuple-element.307), channel_id=1, source_target_pairs={{1,0},{2,1},{3,2},{4,3},{5,4},{6,5},{7,6},{8,7},{9,8},{10,9},{11,1... | collective-permute-start | bytes 589832 | tf_op jit(solution)/shard_map/ppermute | solution.py:28
  67.8 44.6 %copy-start.277 = (f32[4,1024]{1,0:T(4,128)S(1)}, f32[4,1024]{1,0:T(4,128)}, u32[]{:S(2)}) copy-start(f32[4,1024]{1,0:T(4,128)} %fusion.274) | copy-start | bytes 49156
  114.8 49.0 %collective-permute-start.14 = (f32[16,3,1,4,1024]{4,0,3,1,2:T(8,128)S(1)}, f32[16,3,1,4,1024]{4,0,3,1,2:T(8,128)S(1)}, u32[]{:S(2)}, u32[]{:S(2)}) collective-permute-start(f32[16,3,1,4,1024]{4,0,3,1,2:T(8,128)S(1)} %get-tuple-element.490), channel_id=1, source_target_pairs={{48,0},{64,16},{80,32},{96,48},{112,64},{49,1},{65,17},{81,33},{97... | collective-permute-start | bytes 2359304 | tf_op jit(solution)/shard_map/ppermute | solution.py:38
  116.2 47.7 %collective-permute-start.12 = (f32[16,3,1,4,1024]{4,0,3,1,2:T(8,128)S(1)}, f32[16,3,1,4,1024]{4,0,3,1,2:T(8,128)S(1)}, u32[]{:S(2)}, u32[]{:S(2)}) collective-permute-start(f32[16,3,1,4,1024]{4,0,3,1,2:T(8,128)S(1)} %get-tuple-element.490), channel_id=1, source_target_pairs={{16,0},{32,16},{48,32},{64,48},{80,64},{96,80},{112,96},{17,1},{33... | collective-permute-start | bytes 2359304 | tf_op jit(solution)/shard_map/ppermute | solution.py:38
  127.8 24.3 %collective-permute-start.11 = (f32[16,3,1,3,1024]{4,0,3,1,2:T(8,128)S(1)}, f32[16,3,1,3,1024]{4,0,3,1,2:T(8,128)S(1)}, u32[]{:S(2)}, u32[]{:S(2)}) collective-permute-start(f32[16,3,1,3,1024]{4,0,3,1,2:T(8,128)S(1)} %get-tuple-element.276), channel_id=1, source_target_pairs={{0,1},{1,2},{2,3},{3,4},{4,5},{5,6},{6,7},{7,8},{8,9},{9,10},{10,1... | collective-permute-start | bytes 1769480 | tf_op jit(solution)/shard_map/ppermute | solution.py:26
  130.0 8.5 %collective-permute-start.7 = (f32[16,3,1,1,1024]{4,0,3,1,2:T(8,128)S(1)}, f32[16,3,1,1,1024]{4,0,3,1,2:T(8,128)S(1)}, u32[]{:S(2)}, u32[]{:S(2)}) collective-permute-start(f32[16,3,1,1,1024]{4,0,3,1,2:T(8,128)S(1)} %get-tuple-element.291), channel_id=1, source_target_pairs={{1,0},{2,1},{3,2},{4,3},{5,4},{6,5},{7,6},{8,7},{9,8},{10,9},{11,1... | collective-permute-start | bytes 589832 | tf_op jit(solution)/shard_map/ppermute | solution.py:28
  135.4 10.0 %collective-permute-start.8 = (f32[16,3,1,1,1024]{4,0,3,1,2:T(8,128)S(1)}, f32[16,3,1,1,1024]{4,0,3,1,2:T(8,128)S(1)}, u32[]{:S(2)}, u32[]{:S(2)}) collective-permute-start(f32[16,3,1,1,1024]{4,0,3,1,2:T(8,128)S(1)} %get-tuple-element.290), channel_id=1, source_target_pairs={{0,1},{1,2},{2,3},{3,4},{4,5},{5,6},{6,7},{7,8},{8,9},{9,10},{10,1... | collective-permute-start | bytes 589832 | tf_op jit(solution)/shard_map/ppermute | solution.py:26
  138.6 25.6 %collective-permute-start.15 = (f32[16,3,1,4,1024]{4,0,3,1,2:T(8,128)S(1)}, f32[16,3,1,4,1024]{4,0,3,1,2:T(8,128)S(1)}, u32[]{:S(2)}, u32[]{:S(2)}) collective-permute-start(f32[16,3,1,4,1024]{4,0,3,1,2:T(8,128)S(1)} %pad_maximum_fusion.108), channel_id=1, source_target_pairs={{0,48},{16,64},{32,80},{48,96},{64,112},{1,49},{17,65},{33,81},{49... | collective-permute-start | bytes 2359304 | tf_op jit(solution)/shard_map/ppermute | solution.py:38
  145.5 17.7 %collective-permute-start.9 = (f32[16,3,1,3,1024]{4,0,3,1,2:T(8,128)S(1)}, f32[16,3,1,3,1024]{4,0,3,1,2:T(8,128)S(1)}, u32[]{:S(2)}, u32[]{:S(2)}) collective-permute-start(f32[16,3,1,3,1024]{4,0,3,1,2:T(8,128)S(1)} %get-tuple-element.277), channel_id=1, source_target_pairs={{1,0},{2,1},{3,2},{4,3},{5,4},{6,5},{7,6},{8,7},{9,8},{10,9},{11,1... | collective-permute-start | bytes 1769480 | tf_op jit(solution)/shard_map/ppermute | solution.py:28
  152.0 17.2 %collective-permute-start.13 = (f32[16,3,1,4,1024]{4,0,3,1,2:T(8,128)S(1)}, f32[16,3,1,4,1024]{4,0,3,1,2:T(8,128)S(1)}, u32[]{:S(2)}, u32[]{:S(2)}) collective-permute-start(f32[16,3,1,4,1024]{4,0,3,1,2:T(8,128)S(1)} %pad_maximum_fusion.107), channel_id=1, source_target_pairs={{0,16},{16,32},{32,48},{48,64},{64,80},{80,96},{96,112},{1,17},{17... | collective-permute-start | bytes 2359304 | tf_op jit(solution)/shard_map/ppermute | solution.py:38
  173.5 41.5 %collective-permute-start.18 = (f32[16,3,1,4,1024]{4,0,3,1,2:T(8,128)S(1)}, f32[16,3,1,4,1024]{4,0,3,1,2:T(8,128)S(1)}, u32[]{:S(2)}, u32[]{:S(2)}) collective-permute-start(f32[16,3,1,4,1024]{4,0,3,1,2:T(8,128)S(1)} %fusion.79), channel_id=1, source_target_pairs={{16,0},{32,16},{48,32},{64,48},{80,64},{96,80},{112,96},{17,1},{33... | collective-permute-start | bytes 2359304 | tf_op jit(solution)/shard_map/ppermute | solution.py:38
  174.8 40.4 %collective-permute-start.20 = (f32[16,3,1,4,1024]{4,0,3,1,2:T(8,128)S(1)}, f32[16,3,1,4,1024]{4,0,3,1,2:T(8,128)S(1)}, u32[]{:S(2)}, u32[]{:S(2)}) collective-permute-start(f32[16,3,1,4,1024]{4,0,3,1,2:T(8,128)S(1)} %fusion.79), channel_id=1, source_target_pairs={{48,0},{64,16},{80,32},{96,48},{112,64},{49,1},{65,17},{81,33},{97... | collective-permute-start | bytes 2359304 | tf_op jit(solution)/shard_map/ppermute | solution.py:38
  176.3 11.2 %collective-permute-start.16 = (f32[16,3,1,3,1024]{4,0,3,1,2:T(8,128)S(1)}, f32[16,3,1,3,1024]{4,0,3,1,2:T(8,128)S(1)}, u32[]{:S(2)}, u32[]{:S(2)}) collective-permute-start(f32[16,3,1,3,1024]{4,0,3,1,2:T(8,128)S(1)} %get-tuple-element.220), channel_id=1, source_target_pairs={{1,0},{2,1},{3,2},{4,3},{5,4},{6,5},{7,6},{8,7},{9,8},{10,9},{11,1... | collective-permute-start | bytes 1769480 | tf_op jit(solution)/shard_map/ppermute | solution.py:28
  180.0 32.3 %collective-permute-start.17 = (f32[16,3,1,3,1024]{4,0,3,1,2:T(8,128)S(1)}, f32[16,3,1,3,1024]{4,0,3,1,2:T(8,128)S(1)}, u32[]{:S(2)}, u32[]{:S(2)}) collective-permute-start(f32[16,3,1,3,1024]{4,0,3,1,2:T(8,128)S(1)} %get-tuple-element.221), channel_id=1, source_target_pairs={{0,1},{1,2},{2,3},{3,4},{4,5},{5,6},{6,7},{7,8},{8,9},{9,10},{10,1... | collective-permute-start | bytes 1769480 | tf_op jit(solution)/shard_map/ppermute | solution.py:26
  181.5 33.9 %collective-permute-start.19 = (f32[16,3,1,4,1024]{4,0,3,1,2:T(8,128)S(1)}, f32[16,3,1,4,1024]{4,0,3,1,2:T(8,128)S(1)}, u32[]{:S(2)}, u32[]{:S(2)}) collective-permute-start(f32[16,3,1,4,1024]{4,0,3,1,2:T(8,128)S(1)} %pad_maximum_fusion.111), channel_id=1, source_target_pairs={{0,16},{16,32},{32,48},{48,64},{64,80},{80,96},{96,112},{1,17},{17... | collective-permute-start | bytes 2359304 | tf_op jit(solution)/shard_map/ppermute | solution.py:38
  187.4 40.6 %collective-permute-start.21 = (f32[16,3,1,4,1024]{4,0,3,1,2:T(8,128)S(1)}, f32[16,3,1,4,1024]{4,0,3,1,2:T(8,128)S(1)}, u32[]{:S(2)}, u32[]{:S(2)}) collective-permute-start(f32[16,3,1,4,1024]{4,0,3,1,2:T(8,128)S(1)} %pad_maximum_fusion.112), channel_id=1, source_target_pairs={{0,48},{16,64},{32,80},{48,96},{64,112},{1,49},{17,65},{33,81},{49... | collective-permute-start | bytes 2359304 | tf_op jit(solution)/shard_map/ppermute | solution.py:38
  397.2 34.0 %collective-permute-start.26 = (f32[16,3,1,4,1024]{4,0,3,1,2:T(8,128)S(1)}, f32[16,3,1,4,1024]{4,0,3,1,2:T(8,128)S(1)}, u32[]{:S(2)}, u32[]{:S(2)}) collective-permute-start(f32[16,3,1,4,1024]{4,0,3,1,2:T(8,128)S(1)} %multiply_add_fusion.1), channel_id=1, source_target_pairs={{48,0},{64,16},{80,32},{96,48},{112,64},{49,1},{65,17},{81,33},{97... | collective-permute-start | bytes 2359304 | tf_op jit(solution)/shard_map/ppermute | solution.py:38
  399.0 32.3 %collective-permute-start.24 = (f32[16,3,1,4,1024]{4,0,3,1,2:T(8,128)S(1)}, f32[16,3,1,4,1024]{4,0,3,1,2:T(8,128)S(1)}, u32[]{:S(2)}, u32[]{:S(2)}) collective-permute-start(f32[16,3,1,4,1024]{4,0,3,1,2:T(8,128)S(1)} %multiply_add_fusion.1), channel_id=1, source_target_pairs={{16,0},{32,16},{48,32},{64,48},{80,64},{96,80},{112,96},{17,1},{33... | collective-permute-start | bytes 2359304 | tf_op jit(solution)/shard_map/ppermute | solution.py:38
  400.6 30.9 %collective-permute-start.27 = (f32[16,3,1,4,1024]{4,0,3,1,2:T(8,128)S(1)}, f32[16,3,1,4,1024]{4,0,3,1,2:T(8,128)S(1)}, u32[]{:S(2)}, u32[]{:S(2)}) collective-permute-start(f32[16,3,1,4,1024]{4,0,3,1,2:T(8,128)S(1)} %pad_maximum_fusion.116), channel_id=1, source_target_pairs={{0,48},{16,64},{32,80},{48,96},{64,112},{1,49},{17,65},{33,81},{49... | collective-permute-start | bytes 2359304 | tf_op jit(solution)/shard_map/ppermute | solution.py:38
  409.1 14.1 %collective-permute-start.23 = (f32[16,3,1,3,1024]{4,0,3,1,2:T(8,128)S(1)}, f32[16,3,1,3,1024]{4,0,3,1,2:T(8,128)S(1)}, u32[]{:S(2)}, u32[]{:S(2)}) collective-permute-start(f32[16,3,1,3,1024]{4,0,3,1,2:T(8,128)S(1)} %get-tuple-element.212), channel_id=1, source_target_pairs={{0,1},{1,2},{2,3},{3,4},{4,5},{5,6},{6,7},{7,8},{8,9},{9,10},{10,1... | collective-permute-start | bytes 1769480 | tf_op jit(solution)/shard_map/ppermute | solution.py:26
  409.1 21.0 %collective-permute-start.22 = (f32[16,3,1,3,1024]{4,0,3,1,2:T(8,128)S(1)}, f32[16,3,1,3,1024]{4,0,3,1,2:T(8,128)S(1)}, u32[]{:S(2)}, u32[]{:S(2)}) collective-permute-start(f32[16,3,1,3,1024]{4,0,3,1,2:T(8,128)S(1)} %get-tuple-element.213), channel_id=1, source_target_pairs={{1,0},{2,1},{3,2},{4,3},{5,4},{6,5},{7,6},{8,7},{9,8},{10,9},{11,1... | collective-permute-start | bytes 1769480 | tf_op jit(solution)/shard_map/ppermute | solution.py:28
  423.1 15.5 %collective-permute-start.25 = (f32[16,3,1,4,1024]{4,0,3,1,2:T(8,128)S(1)}, f32[16,3,1,4,1024]{4,0,3,1,2:T(8,128)S(1)}, u32[]{:S(2)}, u32[]{:S(2)}) collective-permute-start(f32[16,3,1,4,1024]{4,0,3,1,2:T(8,128)S(1)} %pad_maximum_fusion.115), channel_id=1, source_target_pairs={{0,16},{16,32},{32,48},{48,64},{64,80},{80,96},{96,112},{1,17},{17... | collective-permute-start | bytes 2359304 | tf_op jit(solution)/shard_map/ppermute | solution.py:38
  443.1 54.4 %collective-permute-start.32 = (f32[16,3,1,4,1024]{4,0,3,1,2:T(8,128)S(1)}, f32[16,3,1,4,1024]{4,0,3,1,2:T(8,128)S(1)}, u32[]{:S(2)}, u32[]{:S(2)}) collective-permute-start(f32[16,3,1,4,1024]{4,0,3,1,2:T(8,128)S(1)} %fusion.32), channel_id=1, source_target_pairs={{48,0},{64,16},{80,32},{96,48},{112,64},{49,1},{65,17},{81,33},{97... | collective-permute-start | bytes 2359304 | tf_op jit(solution)/shard_map/ppermute | solution.py:38
  444.5 53.1 %collective-permute-start.30 = (f32[16,3,1,4,1024]{4,0,3,1,2:T(8,128)S(1)}, f32[16,3,1,4,1024]{4,0,3,1,2:T(8,128)S(1)}, u32[]{:S(2)}, u32[]{:S(2)}) collective-permute-start(f32[16,3,1,4,1024]{4,0,3,1,2:T(8,128)S(1)} %fusion.32), channel_id=1, source_target_pairs={{16,0},{32,16},{48,32},{64,48},{80,64},{96,80},{112,96},{17,1},{33... | collective-permute-start | bytes 2359304 | tf_op jit(solution)/shard_map/ppermute | solution.py:38
  445.8 43.3 %collective-permute-start.28 = (f32[16,3,1,3,1024]{4,0,3,1,2:T(8,128)S(1)}, f32[16,3,1,3,1024]{4,0,3,1,2:T(8,128)S(1)}, u32[]{:S(2)}, u32[]{:S(2)}) collective-permute-start(f32[16,3,1,3,1024]{4,0,3,1,2:T(8,128)S(1)} %get-tuple-element.156), channel_id=1, source_target_pairs={{1,0},{2,1},{3,2},{4,3},{5,4},{6,5},{7,6},{8,7},{9,8},{10,9},{11,1... | collective-permute-start | bytes 1769480 | tf_op jit(solution)/shard_map/ppermute | solution.py:28
  445.9 50.3 %collective-permute-start.29 = (f32[16,3,1,3,1024]{4,0,3,1,2:T(8,128)S(1)}, f32[16,3,1,3,1024]{4,0,3,1,2:T(8,128)S(1)}, u32[]{:S(2)}, u32[]{:S(2)}) collective-permute-start(f32[16,3,1,3,1024]{4,0,3,1,2:T(8,128)S(1)} %get-tuple-element.157), channel_id=1, source_target_pairs={{0,1},{1,2},{2,3},{3,4},{4,5},{5,6},{6,7},{7,8},{8,9},{9,10},{10,1... | collective-permute-start | bytes 1769480 | tf_op jit(solution)/shard_map/ppermute | solution.py:26
  482.8 19.4 %collective-permute-start.31 = (f32[16,3,1,4,1024]{4,0,3,1,2:T(8,128)S(1)}, f32[16,3,1,4,1024]{4,0,3,1,2:T(8,128)S(1)}, u32[]{:S(2)}, u32[]{:S(2)}) collective-permute-start(f32[16,3,1,4,1024]{4,0,3,1,2:T(8,128)S(1)} %pad_maximum_fusion.119), channel_id=1, source_target_pairs={{0,16},{16,32},{32,48},{48,64},{64,80},{80,96},{96,112},{1,17},{17... | collective-permute-start | bytes 2359304 | tf_op jit(solution)/shard_map/ppermute | solution.py:38
  489.2 16.3 %collective-permute-start.33 = (f32[16,3,1,4,1024]{4,0,3,1,2:T(8,128)S(1)}, f32[16,3,1,4,1024]{4,0,3,1,2:T(8,128)S(1)}, u32[]{:S(2)}, u32[]{:S(2)}) collective-permute-start(f32[16,3,1,4,1024]{4,0,3,1,2:T(8,128)S(1)} %pad_maximum_fusion.120), channel_id=1, source_target_pairs={{0,48},{16,64},{32,80},{48,96},{64,112},{1,49},{17,65},{33,81},{49... | collective-permute-start | bytes 2359304 | tf_op jit(solution)/shard_map/ppermute | solution.py:38
  621.6 44.4 %all-to-all-start = ((f32[8,1,24576]{2,1,0:T(1,128)}), f32[8,1,24576]{2,1,0:T(1,128)S(1)}, u32[]{:S(2)}, u32[]{:S(2)}) async-start(f32[8,1,24576]{2,1,0:T(1,128)} %reshape.7396), calls=%async_computation | async-start | bytes 1572864 | tf_op jit(solution)/shard_map/all_to_all | solution.py:229
  (285 other events, 1111.3 us)
where the time goes:
time: 702 us; the launch traced here: 690 us
  blocking collectives  336 us (48%)
  starting transfers between devices  153 us (22%)
  local copies, waits for them, and re-layouts  69.6 us (10%)
  other arithmetic  67.4 us (10%)
  waiting for transfers between devices  52.5 us (7%)
    psum x3, blocking collectives, lattice_sum(): return lax.psum(values, ('tm', 'space'))  262 us
    ppermute x16, starting transfers between devices, from_behind(): lax.ppermute(value, axis, [(source, source + steps) for source in range(l...  77 us
    psum x2, blocking collectives, space_sum(): return lax.psum(values, 'space')  74.7 us
    ppermute x10, starting transfers between devices, extended_2(): lax.ppermute(tail, axis, [(i, (i + 1) % count) for i in range(count)])  40.3 us
    ppermute x16, waiting for transfers between devices, from_behind(): lax.ppermute(value, axis, [(source, source + steps) for source in range(l...  32.5 us
    ppermute x8, starting transfers between devices, extended_2(): lax.ppermute(head, axis, [((i + 1) % count, i) for i in range(count)])  32.1 us
    unnamed x602, local copies, waits for them, and re-layouts  21.6 us
    ppermute x10, waiting for transfers between devices, extended_2(): lax.ppermute(tail, axis, [(i, (i + 1) % count) for i in range(count)])  14.4 us
  transfers between devices with their start and end apart: 35, of which 11 were waited for; matrix products, arithmetic and copies ran while one was open for 9% of the time, Pallas kernels for 0%

commit v1 on v0

v1 whole, which is shorter than its diff:
```python
import functools
import jax
import jax.numpy as jnp
from jax import lax
from jax.sharding import PartitionSpec as P
import jax.experimental.pallas as pl
import jax.experimental.pallas.tpu as pltpu

MESH = pl.DeviceIdType.MESH
HIGH = lax.Precision.HIGHEST
F32 = jnp.float32
CENTER = 6.5
HALF_WIDTH = 5.5
ONE_HOP = 1.125
THREE_HOP = -1.0 / 24.0
SITES = 196608.0

ZP, ZM, PK, SKL, SUB, DSK, DSKS, CC, CT1, CT3, CZ1, CZ3, ZZ, EX, SLOTS = (
    0, 1, 2, 4, 5, 6, 7, 8, 10, 12, 14, 16, 18, 26, 28)


def lanes(v, idx):
    return jnp.take_along_axis(v, idx, axis=1, mode="promise_in_bounds")


def rows(v, idx):
    return jnp.take_along_axis(v, idx, axis=0, mode="promise_in_bounds")


def tile_iota():
    row = lax.broadcasted_iota(jnp.int32, (8, 128), 0)
    lane = lax.broadcasted_iota(jnp.int32, (8, 128), 1)
    return row, lane


def mul_add(acc, links, field, back):
    out = []
    for a in range(3):
        total = acc[a]
        for b in range(3):
            total = total + links[b * 3 + a if back else a * 3 + b] * field[b]
        out.append(total)
    return out


def fill_positions(ix, t):
    row, lane = tile_iota()
    chunk = lane >> 4
    low = lane & 15
    zc = lane & 7
    ix[ZP] = (chunk << 4) | ((low + 1) & 15)
    ix[ZM] = (chunk << 4) | ((low - 1) & 15)
    ysrc = (chunk - t) & 7
    for par in range(2):
        ix[PK + par] = (ysrc << 4) | (zc << 1) | ((t + par + ysrc) & 1)
    ix[SKL] = (((chunk - row) & 7) << 4) | low
    ix[SUB] = (chunk - row) & 7
    ix[DSK] = (((chunk + row) & 7) << 4) | low
    ix[DSKS] = (((chunk + row) & 7) << 4) | (low ^ 8)
    for rho in range(2):
        z = (zc << 1) | ((chunk + row + rho) & 1)
        ix[CC + rho] = (((chunk + row) & 7) << 4) | z
        ix[CT1 + rho] = (((chunk + row - 1) & 7) << 4) | z
        ix[CT3 + rho] = (((chunk + row - 3) & 7) << 4) | z
        ix[CZ1 + rho] = (((chunk + row) & 7) << 4) | ((z - 1) & 15)
        ix[CZ3 + rho] = (((chunk + row) & 7) << 4) | ((z - 3) & 15)
        for j, d in enumerate((1, -1, 3, -3)):
            ix[ZZ + rho * 4 + j] = (lane & 120) | (((z + d) & 15) >> 1)
    ix[EX] = (chunk << 4) | (low >> 1)
    ix[EX + 1] = (chunk << 4) | 8 | (low >> 1)


def kernel(start_ref, smear_ref, fat_ref, naik_ref, proj_ref, out_ref,
           raw, sraw, yy, sx, syz, hh, af, prod, fs, fr, lraw, lxh, lyh, tl, tx, tyh, ll,
           ee, hn, hp, h2, fp, fps, ix, cb, mom, gone, gslot, gtm, kone, kslot, sone, sslot, stm,
           in_sem, y_send, y_recv, sx_send, sx_recv, l_send, l_recv, l_own, lh_send, lh_recv,
           f_send, f_recv, f_own, dx_send, dx_recv, dy_send, dy_recv,
           c_send, c_recv, r_send, r_recv, t_send, t_recv):
    t = lax.axis_index("tm")
    s = lax.axis_index("space")
    core = s & 1
    chip = s >> 1
    nxt = (t, (s + 1) & 15)
    prv = (t, (s + 15) & 15)
    ynxt = ((t + 1) & 7, s)
    yprv = ((t + 7) & 7, s)
    partner = (t, s + 1 - 2 * core)
    chips = [(t, (s + 2 * j) & 15) for j in range(1, 8)]
    times = [((t + d) & 7, s) for d in range(1, 8)]

    def remote(src, dst, send, recv, dev):
        return pltpu.make_async_remote_copy(src, dst, send, recv, device_id=dev, device_id_type=MESH)

    load_start = pltpu.make_async_copy(start_ref, raw, in_sem.at[0])
    load_smear = pltpu.make_async_copy(smear_ref, sraw, in_sem.at[1])
    load_start.start()
    load_smear.start()
    own_links = [
        pltpu.make_async_copy(ref.at[:, t], lraw.at[t, pl.ds(36 * i, 36)], l_own.at[i])
        for i, ref in enumerate((fat_ref, naik_ref))
    ]
    for c in own_links:
        c.start()

    barrier = pltpu.get_barrier_semaphore()
    friends = [nxt, prv] + chips + times
    for dev in friends:
        pl.semaphore_signal(barrier, inc=1, device_id=dev, device_id_type=MESH)

    fill_positions(ix, t)
    row, lane = tile_iota()
    high_half = (lane & 8) != 0

    load_start.wait()

    def place_start(i, _):
        for x in range(4):
            yy[0, 1 + x, i] = raw[pl.ds(i * 32 + x, 8, stride=4), :]
        return 0

    lax.fori_loop(0, 48, place_start, 0, unroll=4)
    pl.semaphore_wait(barrier, len(friends))

    def halo(n):
        return [
            remote(yy.at[n, 4], yy.at[n, 0], y_send.at[n, 0], y_recv.at[n, 0], nxt),
            remote(yy.at[n, 1], yy.at[n, 5], y_send.at[n, 1], y_recv.at[n, 1], prv),
        ]

    halos = halo(0)
    for c in halos:
        c.start()

    load_smear.wait()

    def ahead_y(v):
        r = pltpu.roll(v, 112, 1)
        return jnp.where(lane < 112, r, pltpu.roll(r, 7, 0))

    def behind_y(v):
        r = pltpu.roll(v, 16, 1)
        return jnp.where(lane >= 16, r, pltpu.roll(r, 1, 0))

    zp_i = ix[ZP]
    zm_i = ix[ZM]

    def place_smear(i, _):
        for x in range(4):
            sx[1 + x, i] = sraw[pl.ds(i * 32 + x, 8, stride=4), :]
            ly = sraw[pl.ds((9 + i) * 32 + x, 8, stride=4), :]
            lz = sraw[pl.ds((18 + i) * 32 + x, 8, stride=4), :]
            syz[x, 0, i] = ly
            syz[x, 1, i] = behind_y(ly)
            syz[x, 2, i] = lz
            syz[x, 3, i] = lanes(lz, zm_i)
        return 0

    lax.fori_loop(0, 9, place_smear, 0)
    sx_copy = remote(sx.at[4], sx.at[0], sx_send, sx_recv, nxt)
    sx_copy.start()

    link_copies = []
    for d in range(1, 8):
        dest = (t + d) & 7
        for i, ref in enumerate((fat_ref, naik_ref)):
            c = remote(ref.at[:, dest], lraw.at[t, pl.ds(36 * i, 36)],
                       l_send.at[i, d - 1], l_recv.at[i, d - 1], (dest, s))
            c.start()
            link_copies.append(c)

    def local_pass(n):
        def step(i, _):
            x = i >> 2
            base = (i & 3) * 12
            field = [[yy[n, 1 + x, base + v * 3 + c] for c in range(3)] for v in range(4)]
            acc = [[jnp.zeros((8, 128), F32)] * 3 for _ in range(4)]
            for d in range(4):
                links = [syz[x, d, e] for e in range(9)]
                for v in range(4):
                    if d == 0:
                        moved = [ahead_y(f) for f in field[v]]
                    elif d == 1:
                        moved = [behind_y(f) for f in field[v]]
                    else:
                        moved = [lanes(f, zp_i if d == 2 else zm_i) for f in field[v]]
                    acc[v] = mul_add(acc[v], links, moved, d & 1)
            for v in range(4):
                for c in range(3):
                    hh[x, base + v * 3 + c] = acc[v][c]
            return 0

        lax.fori_loop(0, 16, step, 0)

    def x_pass(n, plane_of, count, finish):
        def step(i, _):
            x = plane_of(i >> 2)
            base = (i & 3) * 12
            for back in (False, True):
                links = [sx[x if back else 1 + x, e] for e in range(9)]
                for v in range(4):
                    field = [yy[n, x if back else 2 + x, base + v * 3 + c] for c in range(3)]
                    acc = [hh[x, base + v * 3 + c] for c in range(3)] if not back else keep[v]
                    acc = mul_add(acc, links, field, back)
                    if not back:
                        if v == 0:
                            keep = []
                        keep.append(acc)
                    else:
                        for c in range(3):
                            finish(x, base + v * 3 + c, acc[c])
            return 0

        lax.fori_loop(0, 4 * count, step, 0)

    for n in range(3):
        local_pass(n)
        if n == 0:
            sx_copy.wait()
        for c in halos:
            c.wait()

        def finish(x, comp, acc, n=n):
            if n == 0:
                value = (-0.5 / HALF_WIDTH) * yy[0, 1 + x, comp] - (1.0 / HALF_WIDTH) * acc
            else:
                value = ((-1.0 / HALF_WIDTH) * yy[n, 1 + x, comp] - (2.0 / HALF_WIDTH) * acc
                         - yy[n - 1, 1 + x, comp])
            yy[n + 1, 1 + x, comp] = value

        x_pass(n, lambda i: 3 * i, 2, finish)
        if n < 2:
            halos = halo(n + 1)
            for c in halos:
                c.start()
        x_pass(n, lambda i: 1 + i, 2, finish)
        if n == 1:
            for c in own_links + link_copies:
                c.wait()
            link_halos = []
            for i in range(2):
                link_halos.append(remote(lraw.at[:, pl.ds(36 * i, 9)], lxh.at[:, pl.ds(9 * i, 9)],
                                         lh_send.at[0, i], lh_recv.at[0, i], nxt))
                link_halos.append(remote(lraw.at[:, pl.ds(36 * i + 9, 9)], lyh.at[:, pl.ds(9 * i, 9)],
                                         lh_send.at[1, i], lh_recv.at[1, i], ynxt))
            for c in link_halos:
                c.start()

    def pack(i, _):
        x = i >> 3
        pair = i & 7
        idx = ix[PK + (x & 1)]
        for c in range(3):
            one = lanes(yy[3, 1 + x, pair * 3 + c], idx)
            two = lanes(yy[3, 1 + x, pair * 3 + 24 + c], idx)
            fs[pl.ds(x * 24 + pair * 3 + c, 8, stride=96), :] = jnp.where(high_half, two, one)
        return 0

    lax.fori_loop(0, 32, pack, 0)

    def part(ref, which):
        return ref.at[pl.ds(pl.multiple_of(which * 96, 96), 96)]

    f_copies = [
        remote(part(fs, (t + d) & 7), part(fr, t), f_send.at[d - 1], f_recv.at[d - 1], times[d - 1])
        for d in range(1, 8)
    ]
    for c in f_copies:
        c.start()
    f_local = pltpu.make_async_copy(part(fs, t), part(fr, t), f_own)
    f_local.start()

    def products(left, right):
        def step(k, _):
            mine = [left(x, k * 3 + c) for x in range(4) for c in range(3)]
            for d in range(9):
                j = (k + d) & 15
                total = None
                for x in range(4):
                    for c in range(3):
                        term = mine[x * 3 + c] * right(x, j * 3 + c)
                        total = term if total is None else total + term
                total = jnp.sum(total, axis=0, keepdims=True)
                prod[pl.ds(j * 16 + k, 1), :] = total
                prod[pl.ds(k * 16 + j, 1), :] = total
            return 0

        lax.fori_loop(0, 16, step, 0)
        sums = lax.dot_general(jnp.ones((8, 128), F32), prod[...], (((1,), (1,)), ((), ())),
                               precision=HIGH, preferred_element_type=F32)
        return jnp.where(row == 0, sums[:, :128], sums[:, 128:])

    def to_partner(buf, which):
        return remote(buf.at[0], buf.at[1], c_send.at[which], c_recv.at[which], partner)

    def to_chips(buf, which):
        return [remote(buf.at[chip], buf.at[chip], r_send.at[which, j], r_recv.at[which, j], chips[j])
                for j in range(7)]

    def to_times(buf, which):
        return [remote(buf.at[t], buf.at[t], t_send.at[which, j], t_recv.at[which, j], times[j])
                for j in range(7)]

    def total_of(buf):
        total = buf[0]
        for j in range(1, 8):
            total = total + buf[j]
        return total

    gone[0] = products(lambda x, e: yy[3, 1 + x, e], lambda x, e: yy[3, 1 + x, e])
    g_partner = to_partner(gone, 0)
    g_partner.start()
    halos = halo(3)
    for c in halos:
        c.start()

    def turned(ref, first, stride):
        v = lanes(ref[pl.ds(first, 8, stride=stride), :], ix[SKL])
        return rows(v, ix[SUB])

    lflat = lraw.reshape(8 * 72 * 4, 128)
    xflat = lxh.reshape(8 * 18 * 4, 128)
    yflat = lyh.reshape(8 * 18 * 4, 128)

    def place_links(i, _):
        for x in range(4):
            tl[x, i] = turned(lflat, i * 4 + x, 288)
        return 0

    lax.fori_loop(0, 72, place_links, 0)
    g_partner.wait()
    gslot[chip] = gone[0] + gone[1]
    g_chips = to_chips(gslot, 0)
    for c in g_chips:
        c.start()

    for c in link_halos:
        c.wait()

    def place_link_halos(i, _):
        for x in range(4):
            tx[x, i] = turned(xflat, i * 4 + x, 72)
            tyh[x, i] = turned(yflat, i * 4 + x, 72)
        return 0

    lax.fori_loop(0, 18, place_link_halos, 0)
    for c in g_chips:
        c.wait()
    gtm[t] = total_of(gslot)
    g_times = to_times(gtm, 0)
    for c in g_times:
        c.start()

    chunk = lane >> 4

    def fill_links(i, _):
        x = i & 3
        e = i >> 2
        xsign = (1 - 2 * (x & 1)).astype(F32)
        ysign = (1 - 2 * (row & 1)).astype(F32)
        tsign = (1 - 2 * (chunk & 1)).astype(F32)
        for kind, hop, weight in ((0, 1, 0.5 * ONE_HOP), (1, 3, 0.5 * THREE_HOP)):
            off = 36 * kind
            px = x - hop
            own = [tl[x, off + 9 * mu + e] for mu in range(4)]
            before_x = jnp.where(px >= 0, tl[jnp.maximum(px, 0), off + e],
                                 tx[jnp.minimum(px + 4, 3), 9 * kind + e])
            before_y = pltpu.roll(jnp.where(row < 8 - hop, own[1], tyh[x, 9 * kind + e]), hop, 0)
            for pi in range(2):
                rho = (x + pi) & 1
                cc = ix[CC + rho]
                ct = ix[(CT3 if kind else CT1) + rho]
                cz = ix[(CZ3 if kind else CZ1) + rho]
                pis = -1.0 if pi else 1.0
                scale = [
                    jnp.full((8, 128), weight, F32),
                    jnp.full((8, 128), weight, F32) * xsign,
                    weight * xsign * ysign,
                ]
                fwd = [lanes(own[mu], cc) for mu in range(4)]
                bwd = [lanes(before_x, cc), lanes(before_y, ct), lanes(own[2], cz), lanes(own[3], ct)]
                for mu in range(4):
                    if mu < 3:
                        up, down = scale[mu], -scale[mu]
                    else:
                        up = jnp.where(chunk < 8 - hop, (pis * weight) * tsign, 0.0)
                        down = jnp.where(chunk >= hop, (-pis * weight) * tsign, 0.0)
                    ll[pi, x, (mu * 2 + kind) * 2, e] = up * fwd[mu]
                    ll[pi, x, (mu * 2 + kind) * 2 + 1, e] = down * bwd[mu]
        return 0

    lax.fori_loop(0, 36, fill_links, 0)

    for c in f_copies:
        c.wait()
    f_local.wait()

    def unpack(i, _):
        x = i >> 3
        for c in range(3):
            e = (i & 7) * 3 + c
            v = rows(fr[pl.ds(x * 24 + e, 8, stride=96), :], ix[SUB])
            fp[x, e] = lanes(v, ix[DSK])
            fps[x, e] = lanes(v, ix[DSKS])
        return 0

    lax.fori_loop(0, 32, unpack, 0)

    for c in g_times:
        c.wait()

    flat = gtm.reshape(64, 128)
    expand = jnp.where(chunk == row, 1.0 / SITES, 0.0).astype(F32)
    for half in range(2):
        cb[pl.ds(128 * half, 128), :] = lax.dot_general(
            flat[pl.ds(half, 8, stride=8), :], jnp.where(chunk == row, 1.0, 0.0).astype(F32),
            (((0,), (0,)), ((), ())), precision=HIGH, preferred_element_type=F32)
    cols = [cb[pl.ds(16 * m, 16), :] * (1.0 / SITES) for m in range(16)]
    line = lax.broadcasted_iota(jnp.int32, (16, 128), 0)
    inv = [jnp.where(line == m, 1.0, 0.0).astype(F32) for m in range(16)]
    for j in range(16):
        scale = 1.0 / jnp.sqrt(cols[j][j:j + 1])
        factor = jnp.where(line > j, cols[j] * scale, 0.0)
        for m in range(j + 1, 16):
            cols[m] = cols[m] - factor * (cols[m][j:j + 1] * scale)
        for m in range(j + 1):
            top = inv[m][j:j + 1] * scale
            inv[m] = jnp.where(line == j, top, inv[m] - factor * top)
    for m in range(16):
        cb[pl.ds(16 * m, 16), :] = inv[m]

    def entry(k, j):
        return jnp.broadcast_to(cb[pl.ds(16 * j + k, 1), :], (8, 128))

    for pair in range(8):
        same = [jnp.where(high_half, entry(pair + 8, j + 8), entry(pair, j)) for j in range(pair + 1)]
        cross = [jnp.where(high_half, entry(pair + 8, j), 0.0) for j in range(8)]

        def mix(x, total, pair=pair, same=same, cross=cross):
            for c in range(3):
                value = cross[0] * fps[x, c]
                for j in range(1, 8):
                    value = value + cross[j] * fps[x, j * 3 + c]
                for j in range(pair + 1):
                    value = value + same[j] * fp[x, j * 3 + c]
                ee[0, 3 + x, pair * 3 + c] = value
                total = total + value * value
            return total

        mom[0, pair] = lax.fori_loop(0, 4, mix, jnp.zeros((8, 128), F32))

    def d_halo(n):
        return [
            remote(ee.at[n, pl.ds(4, 3)], ee.at[n, pl.ds(0, 3)], dx_send.at[n, 0], dx_recv.at[n, 0], nxt),
            remote(ee.at[n, pl.ds(3, 3)], ee.at[n, pl.ds(7, 3)], dx_send.at[n, 1], dx_recv.at[n, 1], prv),
            remote(ee.at[n, pl.ds(3, 4), :, pl.ds(5, 3)], hp.at[n, :, :, pl.ds(5, 3)],
                   dy_send.at[n, 0], dy_recv.at[n, 0], ynxt),
            remote(ee.at[n, pl.ds(3, 4), :, pl.ds(0, 3)], hn.at[n, :, :, pl.ds(0, 3)],
                   dy_send.at[n, 1], dy_recv.at[n, 1], yprv),
        ]

    def inner_pass(n, pi):
        def step(i, _):
            x = i >> 1
            base = (i & 1) * 12
            rho = (x + pi) & 1
            field = [[ee[n, 3 + x, base + v * 3 + c] for c in range(3)] for v in range(4)]
            acc = [[jnp.zeros((8, 128), F32)] * 3 for _ in range(4)]
            for d in range(8, 16):
                links = [ll[pi, x, d, e] for e in range(9)]
                hop = 3 if (d >> 1) & 1 else 1
                if d < 12:
                    idx = ix[ZZ + rho * 4 + (d - 8)]
                for v in range(4):
                    if d < 12:
                        moved = [lanes(f, idx) for f in field[v]]
                    else:
                        shift = 16 * hop if d & 1 else 128 - 16 * hop
                        moved = [pltpu.roll(f, shift, 1) for f in field[v]]
                    acc[v] = mul_add(acc[v], links, moved, d & 1)
            for v in range(4):
                for c in range(3):
                    h2[x, base + v * 3 + c] = acc[v][c]
            return 0

        lax.fori_loop(0, 8, step, 0)

    def outer_pass(n, pi, store):
        for pair in range(8):
            mom[n + 1, pair] = jnp.zeros((8, 128), F32)

        def step(i, _):
            x = i >> 1
            base = (i & 1) * 12
            acc = [[h2[x, base + v * 3 + c] for c in range(3)] for v in range(4)]
            for d in range(8):
                links = [ll[pi, x, d, e] for e in range(9)]
                hop = 3 if (d >> 1) & 1 else 1
                for v in range(4):
                    comps = [base + v * 3 + c for c in range(3)]
                    if d < 4:
                        moved = [ee[n, 3 + x - hop if d & 1 else 3 + x + hop, e] for e in comps]
                    elif d & 1:
                        moved = [pltpu.roll(jnp.where(row < 8 - hop, ee[n, 3 + x, e], hp[n, x, e]), hop, 0)
                                 for e in comps]
                    else:
                        moved = [pltpu.roll(jnp.where(row >= hop, ee[n, 3 + x, e], hn[n, x, e]), 8 - hop, 0)
                                 for e in comps]
                    acc[v] = mul_add(acc[v], links, moved, d & 1)
            for v in range(4):
                for c in range(3):
                    if store:
                        ee[n + 1, 3 + x, base + v * 3 + c] = acc[v][c]
                mom[n + 1, (i & 1) * 4 + v] += (
                    acc[v][0] * acc[v][0] + acc[v][1] * acc[v][1] + acc[v][2] * acc[v][2])
            return 0

        lax.fori_loop(0, 8, step, 0)

    def flat_to_square(tile):
        total = jnp.zeros((16, 128), F32)
        for m in range(16):
            piece = jnp.broadcast_to(tile[m >> 3:(m >> 3) + 1], (16, 128))
            piece = pltpu.roll(piece, (128 - 16 * (m & 7)) & 127, 1) if m & 7 else piece
            total = jnp.where(line == m, piece, total)
        return total[:, :16]

    for n in range(3):
        pi = 1 - (n & 1)
        d_copies = d_halo(n)
        for c in d_copies:
            c.start()
        inner_pass(n, pi)
        if n == 0:
            local_pass(3)
            for c in halos:
                c.wait()

            def keep_image(x, comp, acc):
                af[x, comp] = 6.0 * yy[3, 1 + x, comp] - acc

            x_pass(3, lambda i: i, 4, keep_image)
            kone[0] = products(lambda x, e: yy[3, 1 + x, e], lambda x, e: af[x, e])
            k_partner = to_partner(kone, 1)
            k_partner.start()
        if n == 1:
            k_partner.wait()
            kslot[chip] = kone[0] + kone[1]
            k_chips = to_chips(kslot, 1)
            for c in k_chips:
                c.start()
        if n == 2:
            for c in k_chips:
                c.wait()
            square = flat_to_square(total_of(kslot)) * (1.0 / SITES)
            pick = jnp.where(lane == t * 16, 1.0, 0.0).astype(F32)
            weights = lax.dot_general(pick, cb[...], (((1,), (1,)), ((), ())),
                                      precision=HIGH, preferred_element_type=F32)
            weights = flat_to_square(jnp.where(row == 0, weights[:, :128], weights[:, 128:]))
            half = lax.dot_general(weights, square, (((0,), (0,)), ((), ())),
                                   precision=HIGH, preferred_element_type=F32)
            proj_ref[0] = lax.dot_general(half, weights, (((1,), (0,)), ((), ())),
                                          precision=HIGH, preferred_element_type=F32)
        for c in d_copies:
            c.wait()
        outer_pass(n, pi, n < 2)

    prod[...] = jnp.zeros((256, 128), F32)
    for m in range(4):
        for pair in range(8):
            prod[pl.ds(8 * m + pair, 1), :] = jnp.sum(mom[m, pair], axis=0, keepdims=True)
    select = jnp.where(((lane >> 3) & 1) == row, 1.0, 0.0).astype(F32)
    sone[0] = lax.dot_general(select, prod[pl.ds(0, 128), :], (((1,), (1,)), ((), ())),
                              precision=HIGH, preferred_element_type=F32)
    s_partner = to_partner(sone, 2)
    s_partner.start()
    s_partner.wait()
    sslot[chip] = sone[0] + sone[1]
    s_chips = to_chips(sslot, 2)
    for c in s_chips:
        c.start()
    for c in s_chips:
        c.wait()
    stm[t] = total_of(sslot)
    s_times = to_times(stm, 1)
    for c in s_times:
        c.start()
    for c in s_times:
        c.wait()
    n0 = total_of(stm)
    n1 = pltpu.roll(n0, 120, 1)
    n2 = pltpu.roll(n0, 112, 1)
    n3 = pltpu.roll(n0, 104, 1)
    ratio = n1 / n0
    alpha0 = 1.0 / (0.25 + ratio)
    rr = alpha0 * alpha0 * (n2 - ratio * n1)
    beta = rr / n0
    a = alpha0 * ratio + beta
    energy = 0.25 * rr * (1.0 + beta) + a * a * n1 - 2.0 * a * alpha0 * n2 + alpha0 * alpha0 * n3
    alpha1 = rr / energy
    first = alpha0 + alpha1 * a
    second = alpha1 * alpha0

    def spread(v, pair):
        low = jnp.broadcast_to(v[0:1, pair:pair + 1], (8, 128))
        high = jnp.broadcast_to(v[1:2, pair:pair + 1], (8, 128))
        return jnp.where(high_half, high, low)

    for pair in range(8):
        ca = spread(first, pair)
        cd = spread(second, pair)

        def finish_out(x, _, pair=pair, ca=ca, cd=cd):
            even = ((x + row + chunk + lane) & 1) == 0
            for c in range(3):
                value = ca * ee[0, 3 + x, pair * 3 + c] + cd * ee[2, 3 + x, pair * 3 + c]
                out_ref[pair, c, x] = jnp.where(even, lanes(value, ix[EX]), 0.0)
                out_ref[pair + 8, c, x] = jnp.where(even, lanes(value, ix[EX + 1]), 0.0)
            return 0

        lax.fori_loop(0, 4, finish_out, 0)


def rows_first(array, lead):
    return array.reshape(lead, 4, 8, 128).transpose(0, 2, 1, 3)


def body(start, smear_links, fat_links, naik_links):
    start = rows_first(start, 48).reshape(1536, 128)
    smear = rows_first(smear_links, 27).reshape(864, 128)
    fat = rows_first(fat_links, 36)
    naik = rows_first(naik_links, 36)
    vm = lambda *shape: pltpu.VMEM(shape, F32)
    dma = lambda *shape: pltpu.SemaphoreType.DMA(shape) if shape else pltpu.SemaphoreType.DMA
    anywhere = pl.BlockSpec(memory_space=pl.ANY)
    local = pl.BlockSpec(memory_space=pltpu.VMEM)
    return pl.pallas_call(
        kernel,
        out_shape=(jax.ShapeDtypeStruct((1, 16, 16), F32),
                   jax.ShapeDtypeStruct((16, 3, 4, 8, 128), F32)),
        in_specs=[anywhere] * 4,
        out_specs=(local, local),
        scratch_shapes=[
            vm(1536, 128), vm(864, 128), vm(4, 6, 48, 8, 128), vm(5, 9, 8, 128), vm(4, 4, 9, 8, 128),
            vm(4, 48, 8, 128), vm(4, 48, 8, 128), vm(256, 128), vm(768, 128), vm(768, 128),
            vm(8, 72, 4, 128), vm(8, 18, 4, 128), vm(8, 18, 4, 128),
            vm(4, 72, 8, 128), vm(4, 18, 8, 128), vm(4, 18, 8, 128), vm(2, 4, 16, 9, 8, 128),
            vm(3, 10, 24, 8, 128), vm(3, 4, 24, 8, 128), vm(3, 4, 24, 8, 128), vm(4, 24, 8, 128),
            vm(4, 24, 8, 128), vm(4, 24, 8, 128), pltpu.VMEM((SLOTS, 8, 128), jnp.int32),
            vm(256, 128), vm(4, 8, 8, 128),
            vm(2, 8, 128), vm(8, 8, 128), vm(8, 8, 128),
            vm(2, 8, 128), vm(8, 8, 128),
            vm(2, 8, 128), vm(8, 8, 128), vm(8, 8, 128),
            dma(2), dma(4, 2), dma(4, 2), dma(), dma(), dma(2, 7), dma(2, 7), dma(2),
            dma(2, 2), dma(2, 2), dma(7), dma(7), dma(),
            dma(3, 2), dma(3, 2), dma(3, 2), dma(3, 2),
            dma(3), dma(3), dma(3, 7), dma(3, 7), dma(2, 7), dma(2, 7),
        ],
        compiler_params=pltpu.CompilerParams(
            collective_id=0, has_side_effects=True, vmem_limit_bytes=40 * 2**20),
        name="distill",
    )(start, smear, fat, naik)


def solution(mesh):
    in_specs = (
        P(None, None, "tm", "space", None),
        P(None, None, None, "tm", "space", None),
        P(None, None, None, "tm", "space", None),
        P(None, None, None, "tm", "space", None),
    )
    out_specs = (P("tm", None, None), P(None, None, "space", "tm", None))
    return jax.shard_map(body, mesh=mesh, in_specs=in_specs, out_specs=out_specs, check_vma=False)
```

time: 702 us -> 130 us (0.19); the launches traced: 690 us -> 129 us
  blocking collectives: 336 us -> 0 us
  starting transfers between devices: 153 us -> 0 us
  Pallas kernels: 0 us -> 123 us
  other arithmetic: 67.4 us -> 0 us
  local copies, waits for them, and re-layouts: 69.6 us -> 5.75 us
  waiting for transfers between devices: 52.5 us -> 0 us
    psum x5 -> x0, blocking collectives: 336 us -> none  [the longest x3 262 us: lattice_sum(): return lax.psum(values, ('tm', 'space'))]
    ppermute x34 -> x0, starting transfers between devices: 149 us -> none  [the longest x16 77 us: from_behind(): lax.ppermute(value, axis, [(source, source + steps) for source in range(l...]
    pallas_call x0 -> x1, Pallas kernels: none -> 123 us  [body(): pl.pallas_call(kernel, out_shape=(jax.ShapeDtypeStruct((1, 16, 16), F32),...]
    ppermute x34 -> x0, waiting for transfers between devices: 52.5 us -> none  [the longest x16 32.5 us: from_behind(): lax.ppermute(value, axis, [(source, source + steps) for source in range(l...]
    add x108 -> x0, other arithmetic: 26.7 us -> none  [the longest x59 13.4 us: turn(): links[a, 0] * field[:, 0] + links[a, 1] * field[:, 1]]
    slice x81 -> x0, local copies, waits for them, and re-layouts: 18.1 us -> none  [the longest x24 5.57 us: shift_z(): ahead = jnp.roll(field, -step, axis=-1)]
    unnamed x602 -> x10, local copies, waits for them, and re-layouts: 21.6 us -> 5.75 us
    mul x8 -> x0, other arithmetic: 11.3 us -> none  [the longest x2 4.71 us: slab_hop(): return 0.5 * total]
  transfers between devices with their start and end apart: 35 -> 0, of which waited for: 11 -> 0; matrix products, arithmetic and copies ran while one was open for 9% -> 0% of each run, Pallas kernels for 0% -> 0%
where the time goes in v1:
time: 130 us; the launch traced here: 129 us
  Pallas kernels  123 us (95%)
  local copies, waits for them, and re-layouts  5.75 us (4%)
    pallas_call x1, Pallas kernels, body(): pl.pallas_call(kernel, out_shape=(jax.ShapeDtypeStruct((1, 16, 16), F32),...  123 us
    unnamed x10, local copies, waits for them, and re-layouts  5.75 us

profile of v1, /device:TPU:0, one launch (start us, length us, event | category | flops | bytes accessed | tf_op | source)
XLA Modules:
  0.0 129.3 jit_solution(122093434423026333)
XLA Ops:
  0.6 0.0 copy-start
  0.6 1.1 copy-done
  1.8 0.0 copy-start.1
  1.8 1.1 copy-done.1
  2.8 0.0 copy-start.2
  2.8 1.1 copy-done.2
  3.9 0.0 copy-start.3
  3.9 1.0 copy-done.3
  4.9 122.9 %distill.1 = (f32[1,16,16]{2,1,0:T(8,128)S(1)}, f32[16,3,4,8,128]{4,3,2,1,0:T(8,128)S(1)}) custom-call(f32[1536,128]{1,0:T(8,128)S(1)} %bitcast.16, f32[864,128]{1,0:T(8,128)S(1)} %bitcast.19, f32[36,8,4,128]{3,2,1,0:T(4,128)S(1)} %bitcast.17, f32[36,8,4,128]{3,2,1,0:T(4,128)S(1)} %bitcast.18), custom_call_target="tpu_custom_call" | custom-call | tf_op jit(solution)/shard_map/distill/pallas_call | solution.py:636
  127.9 0.6 copy.10
  128.5 0.9 copy.11
Async XLA Ops:
  0.6 1.1 copy-start
  1.8 1.1 copy-start.1
  2.8 1.1 copy-start.2
  3.9 1.0 copy-start.3

commit v2 on v1

--- a/solution.py
+++ b/solution.py
@@ -71,7 +71,7 @@
 
 
 def kernel(start_ref, smear_ref, fat_ref, naik_ref, proj_ref, out_ref,
-           raw, sraw, yy, sx, syz, hh, af, prod, fs, fr, lraw, lxh, lyh, tl, tx, tyh, ll,
+           raw, sraw, yy, sx, syz, hh, af, prod, fs, fr, lraw, tl, tx, tyh, ll,
            ee, hn, hp, h2, fp, fps, ix, cb, mom, gone, gslot, gtm, kone, kslot, sone, sslot, stm,
            in_sem, y_send, y_recv, sx_send, sx_recv, l_send, l_recv, l_own, lh_send, lh_recv,
            f_send, f_recv, f_own, dx_send, dx_recv, dy_send, dy_recv,
@@ -96,7 +96,7 @@
     load_start.start()
     load_smear.start()
     own_links = [
-        pltpu.make_async_copy(ref.at[:, t], lraw.at[t, pl.ds(36 * i, 36)], l_own.at[i])
+        pltpu.make_async_copy(ref.at[:, pl.ds(0, 6), t], lraw.at[t, i], l_own.at[i])
         for i, ref in enumerate((fat_ref, naik_ref))
     ]
     for c in own_links:
@@ -163,7 +163,7 @@
     for d in range(1, 8):
         dest = (t + d) & 7
         for i, ref in enumerate((fat_ref, naik_ref)):
-            c = remote(ref.at[:, dest], lraw.at[t, pl.ds(36 * i, 36)],
+            c = remote(ref.at[:, pl.ds(0, 6), dest], lraw.at[t, i],
                        l_send.at[i, d - 1], l_recv.at[i, d - 1], (dest, s))
             c.start()
             link_copies.append(c)
@@ -212,10 +212,39 @@
 
         lax.fori_loop(0, 4 * count, step, 0)
 
+    lflat = lraw.reshape(8 * 192, 128)
+
+    def place_links(i, _):
+        kind = i >> 2
+        mu = i & 3
+        for x in range(4):
+            tiles = []
+            for e in range(6):
+                v = lanes(lflat[pl.ds(i * 24 + e * 4 + x, 8, stride=192), :], ix[SKL])
+                tiles.append(rows(v, ix[SUB]))
+            for a in range(3):
+                b, c = (a + 1) % 3, (a + 2) % 3
+                tiles.append(tiles[b] * tiles[3 + c] - tiles[c] * tiles[3 + b])
+            for e in range(9):
+                tl[x, kind, mu, e] = tiles[e]
+        return 0
+
     for n in range(3):
         local_pass(n)
         if n == 0:
             sx_copy.wait()
+        if n == 2:
+            for c in own_links + link_copies:
+                c.wait()
+            lax.fori_loop(0, 8, place_links, 0)
+            link_halos = [
+                remote(tl.at[3, 0, 0], tx.at[0, 3], lh_send.at[0, 0], lh_recv.at[0, 0], nxt),
+                remote(tl.at[pl.ds(1, 3), 1, 0], tx.at[1, pl.ds(1, 3)], lh_send.at[0, 1], lh_recv.at[0, 1], nxt),
+                remote(tl.at[:, 0, 1, :, pl.ds(7, 1)], tyh.at[0, :, :, pl.ds(7, 1)],
+                       lh_send.at[1, 0], lh_recv.at[1, 0], ynxt),
+                remote(tl.at[:, 1, 1, :, pl.ds(5, 3)], tyh.at[1, :, :, pl.ds(5, 3)],
+                       lh_send.at[1, 1], lh_recv.at[1, 1], ynxt),
+            ]
         for c in halos:
             c.wait()
 
@@ -232,42 +261,10 @@
             halos = halo(n + 1)
             for c in halos:
                 c.start()
-        x_pass(n, lambda i: 1 + i, 2, finish)
-        if n == 1:
-            for c in own_links + link_copies:
-                c.wait()
-            link_halos = []
-            for i in range(2):
-                link_halos.append(remote(lraw.at[:, pl.ds(36 * i, 9)], lxh.at[:, pl.ds(9 * i, 9)],
-                                         lh_send.at[0, i], lh_recv.at[0, i], nxt))
-                link_halos.append(remote(lraw.at[:, pl.ds(36 * i + 9, 9)], lyh.at[:, pl.ds(9 * i, 9)],
-                                         lh_send.at[1, i], lh_recv.at[1, i], ynxt))
+        if n == 2:
             for c in link_halos:
                 c.start()
-
-    def pack(i, _):
-        x = i >> 3
-        pair = i & 7
-        idx = ix[PK + (x & 1)]
-        for c in range(3):
-            one = lanes(yy[3, 1 + x, pair * 3 + c], idx)
-            two = lanes(yy[3, 1 + x, pair * 3 + 24 + c], idx)
-            fs[pl.ds(x * 24 + pair * 3 + c, 8, stride=96), :] = jnp.where(high_half, two, one)
-        return 0
-
-    lax.fori_loop(0, 32, pack, 0)
-
-    def part(ref, which):
-        return ref.at[pl.ds(pl.multiple_of(which * 96, 96), 96)]
-
-    f_copies = [
-        remote(part(fs, (t + d) & 7), part(fr, t), f_send.at[d - 1], f_recv.at[d - 1], times[d - 1])
-        for d in range(1, 8)
-    ]
-    for c in f_copies:
-        c.start()
-    f_local = pltpu.make_async_copy(part(fs, t), part(fr, t), f_own)
-    f_local.start()
+        x_pass(n, lambda i: 1 + i, 2, finish)
 
     def products(left, right):
         def step(k, _):
@@ -309,46 +306,41 @@
     gone[0] = products(lambda x, e: yy[3, 1 + x, e], lambda x, e: yy[3, 1 + x, e])
     g_partner = to_partner(gone, 0)
     g_partner.start()
-    halos = halo(3)
-    for c in halos:
-        c.start()
-
-    def turned(ref, first, stride):
-        v = lanes(ref[pl.ds(first, 8, stride=stride), :], ix[SKL])
-        return rows(v, ix[SUB])
-
-    lflat = lraw.reshape(8 * 72 * 4, 128)
-    xflat = lxh.reshape(8 * 18 * 4, 128)
-    yflat = lyh.reshape(8 * 18 * 4, 128)
-
-    def place_links(i, _):
-        for x in range(4):
-            tl[x, i] = turned(lflat, i * 4 + x, 288)
+    def pack(i, _):
+        x = i >> 3
+        pair = i & 7
+        idx = ix[PK + (x & 1)]
+        for c in range(3):
+            one = lanes(yy[3, 1 + x, pair * 3 + c], idx)
+            two = lanes(yy[3, 1 + x, pair * 3 + 24 + c], idx)
+            fs[pl.ds(x * 24 + pair * 3 + c, 8, stride=96), :] = jnp.where(high_half, two, one)
         return 0
 
-    lax.fori_loop(0, 72, place_links, 0)
+    lax.fori_loop(0, 32, pack, 0)
+
+    def part(ref, which):
+        return ref.at[pl.ds(pl.multiple_of(which * 96, 96), 96)]
+
+    f_copies = [
+        remote(part(fs, (t + d) & 7), part(fr, t), f_send.at[d - 1], f_recv.at[d - 1], times[d - 1])
+        for d in range(1, 8)
+    ]
+    for c in f_copies:
+        c.start()
+    f_local = pltpu.make_async_copy(part(fs, t), part(fr, t), f_own)
+    f_local.start()
+
     g_partner.wait()
     gslot[chip] = gone[0] + gone[1]
     g_chips = to_chips(gslot, 0)
     for c in g_chips:
         c.start()
 
+    halos = halo(3)
+    for c in halos:
+        c.start()
     for c in link_halos:
         c.wait()
-
-    def place_link_halos(i, _):
-        for x in range(4):
-            tx[x, i] = turned(xflat, i * 4 + x, 72)
-            tyh[x, i] = turned(yflat, i * 4 + x, 72)
-        return 0
-
-    lax.fori_loop(0, 18, place_link_halos, 0)
-    for c in g_chips:
-        c.wait()
-    gtm[t] = total_of(gslot)
-    g_times = to_times(gtm, 0)
-    for c in g_times:
-        c.start()
 
     chunk = lane >> 4
 
@@ -359,12 +351,11 @@
         ysign = (1 - 2 * (row & 1)).astype(F32)
         tsign = (1 - 2 * (chunk & 1)).astype(F32)
         for kind, hop, weight in ((0, 1, 0.5 * ONE_HOP), (1, 3, 0.5 * THREE_HOP)):
-            off = 36 * kind
             px = x - hop
-            own = [tl[x, off + 9 * mu + e] for mu in range(4)]
-            before_x = jnp.where(px >= 0, tl[jnp.maximum(px, 0), off + e],
-                                 tx[jnp.minimum(px + 4, 3), 9 * kind + e])
-            before_y = pltpu.roll(jnp.where(row < 8 - hop, own[1], tyh[x, 9 * kind + e]), hop, 0)
+            own = [tl[x, kind, mu, e] for mu in range(4)]
+            before_x = jnp.where(px >= 0, tl[jnp.maximum(px, 0), kind, 0, e],
+                                 tx[kind, jnp.minimum(px + 4, 3), e])
+            before_y = pltpu.roll(jnp.where(row < 8 - hop, own[1], tyh[kind, x, e]), hop, 0)
             for pi in range(2):
                 rho = (x + pi) & 1
                 cc = ix[CC + rho]
@@ -390,26 +381,32 @@
 
     lax.fori_loop(0, 36, fill_links, 0)
 
+    for c in g_chips:
+        c.wait()
+    gtm[t] = total_of(gslot)
+    g_times = to_times(gtm, 0)
+    for c in g_times:
+        c.start()
+
     for c in f_copies:
         c.wait()
     f_local.wait()
 
     def unpack(i, _):
-        x = i >> 3
-        for c in range(3):
-            e = (i & 7) * 3 + c
+        x = i >> 1
+        for c in range(12):
+            e = (i & 1) * 12 + c
             v = rows(fr[pl.ds(x * 24 + e, 8, stride=96), :], ix[SUB])
             fp[x, e] = lanes(v, ix[DSK])
             fps[x, e] = lanes(v, ix[DSKS])
         return 0
 
-    lax.fori_loop(0, 32, unpack, 0)
+    lax.fori_loop(0, 8, unpack, 0)
 
     for c in g_times:
         c.wait()
 
     flat = gtm.reshape(64, 128)
-    expand = jnp.where(chunk == row, 1.0 / SITES, 0.0).astype(F32)
     for half in range(2):
         cb[pl.ds(128 * half, 128), :] = lax.dot_general(
             flat[pl.ds(half, 8, stride=8), :], jnp.where(chunk == row, 1.0, 0.0).astype(F32),
@@ -551,7 +548,7 @@
         if n == 2:
             for c in k_chips:
                 c.wait()
-            square = flat_to_square(total_of(kslot)) * (1.0 / SITES)
+            square = flat_to_square(total_of(kslot))
             pick = jnp.where(lane == t * 16, 1.0, 0.0).astype(F32)
             weights = lax.dot_general(pick, cb[...], (((1,), (1,)), ((), ())),
                                       precision=HIGH, preferred_element_type=F32)
@@ -610,14 +607,13 @@
         cd = spread(second, pair)
 
         def finish_out(x, _, pair=pair, ca=ca, cd=cd):
-            even = ((x + row + chunk + lane) & 1) == 0
             for c in range(3):
                 value = ca * ee[0, 3 + x, pair * 3 + c] + cd * ee[2, 3 + x, pair * 3 + c]
-                out_ref[pair, c, x] = jnp.where(even, lanes(value, ix[EX]), 0.0)
-                out_ref[pair + 8, c, x] = jnp.where(even, lanes(value, ix[EX + 1]), 0.0)
+                out_ref[pair, c, x] = lanes(value, ix[EX])
+                out_ref[pair + 8, c, x] = lanes(value, ix[EX + 1])
             return 0
 
-        lax.fori_loop(0, 4, finish_out, 0)
+        lax.fori_loop(0, 4, finish_out, 0, unroll=True)
 
 
 def rows_first(array, lead):
@@ -627,13 +623,13 @@
 def body(start, smear_links, fat_links, naik_links):
     start = rows_first(start, 48).reshape(1536, 128)
     smear = rows_first(smear_links, 27).reshape(864, 128)
-    fat = rows_first(fat_links, 36)
-    naik = rows_first(naik_links, 36)
+    fat = rows_first(fat_links, 36).reshape(4, 9, 8, 4, 128)
+    naik = rows_first(naik_links, 36).reshape(4, 9, 8, 4, 128)
     vm = lambda *shape: pltpu.VMEM(shape, F32)
     dma = lambda *shape: pltpu.SemaphoreType.DMA(shape) if shape else pltpu.SemaphoreType.DMA
     anywhere = pl.BlockSpec(memory_space=pl.ANY)
     local = pl.BlockSpec(memory_space=pltpu.VMEM)
-    return pl.pallas_call(
+    projected, filled = pl.pallas_call(
         kernel,
         out_shape=(jax.ShapeDtypeStruct((1, 16, 16), F32),
                    jax.ShapeDtypeStruct((16, 3, 4, 8, 128), F32)),
@@ -642,8 +638,8 @@
         scratch_shapes=[
             vm(1536, 128), vm(864, 128), vm(4, 6, 48, 8, 128), vm(5, 9, 8, 128), vm(4, 4, 9, 8, 128),
             vm(4, 48, 8, 128), vm(4, 48, 8, 128), vm(256, 128), vm(768, 128), vm(768, 128),
-            vm(8, 72, 4, 128), vm(8, 18, 4, 128), vm(8, 18, 4, 128),
-            vm(4, 72, 8, 128), vm(4, 18, 8, 128), vm(4, 18, 8, 128), vm(2, 4, 16, 9, 8, 128),
+            vm(8, 2, 4, 6, 4, 128),
+            vm(4, 2, 4, 9, 8, 128), vm(2, 4, 9, 8, 128), vm(2, 4, 9, 8, 128), vm(2, 4, 16, 9, 8, 128),
             vm(3, 10, 24, 8, 128), vm(3, 4, 24, 8, 128), vm(3, 4, 24, 8, 128), vm(4, 24, 8, 128),
             vm(4, 24, 8, 128), vm(4, 24, 8, 128), pltpu.VMEM((SLOTS, 8, 128), jnp.int32),
             vm(256, 128), vm(4, 8, 8, 128),
@@ -656,9 +652,12 @@
             dma(3), dma(3), dma(3, 7), dma(3, 7), dma(2, 7), dma(2, 7),
         ],
         compiler_params=pltpu.CompilerParams(
-            collective_id=0, has_side_effects=True, vmem_limit_bytes=40 * 2**20),
+            collective_id=0, has_side_effects=True, vmem_limit_bytes=60 * 2**20),
         name="distill",
     )(start, smear, fat, naik)
+    place = [lax.broadcasted_iota(jnp.int32, (4, 8, 128), d) for d in range(3)]
+    even = ((place[0] + place[1] + (place[2] >> 4) + place[2]) & 1) == 0
+    return projected * (1.0 / SITES), jnp.where(even, filled, 0.0)
 
 
 def solution(mesh):

time: 130 us -> 109 us (0.84)
  Pallas kernels: 123 us -> 104 us
  local copies, waits for them, and re-layouts: 5.75 us -> 0 us
  other arithmetic: 0 us -> 3.4 us
    pallas_call x1, Pallas kernels: 123 us -> 104 us  [body(): pl.pallas_call(kernel, out_shape=(jax.ShapeDtypeStruct((1, 16, 16), F32),...]
    unnamed x10 -> x0, local copies, waits for them, and re-layouts: 5.75 us -> none
    select_n x0 -> x1, other arithmetic: none -> 2.08 us  [body(): return (projected * (1.0 / SITES), jnp.where(even, filled, 0.0))]
where the time goes in v2:
time: 109 us; the launch traced here: 108 us
  Pallas kernels  104 us (95%)
  other arithmetic  3.4 us (3%)
    pallas_call x1, Pallas kernels, body(): pl.pallas_call(kernel, out_shape=(jax.ShapeDtypeStruct((1, 16, 16), F32),...  104 us

profile of v2, /device:TPU:0, one launch (start us, length us, event | category | flops | bytes accessed | tf_op | source)
XLA Modules:
  0.0 108.3 jit_solution(13483331442190004361)
XLA Ops:
  0.7 104.2 %distill.1 = (f32[1,16,16]{2,1,0:T(8,128)}, f32[16,3,4,8,128]{4,3,2,1,0:T(8,128)}) custom-call(f32[1536,128]{1,0:T(8,128)} %bitcast.20, f32[864,128]{1,0:T(8,128)} %bitcast.23, f32[4,9,8,4,128]{4,3,2,1,0:T(4,128)} %bitcast.21, f32[4,9,8,4,128]{4,3,2,1,0:T(4,128)} %bitcast.22), custom_call_target="tpu_custom_call" | custom-call | tf_op jit(solution)/shard_map/distill/pallas_call | solution.py:632
  104.9 1.3 %broadcast_multiply_fusion = f32[1,16,16]{2,1,0:T(8,128)} fusion(f32[1,16,16]{2,1,0:T(8,128)} %get-tuple-element.4), kind=kLoop, calls=%fused_computation.2 | loop fusion | flops 256 | bytes 2048 | tf_op jit(solution)/shard_map/mul | solution.py:660
  106.2 2.1 %broadcast_select_fusion = f32[16,3,4,8,128]{4,3,2,1,0:T(8,128)} fusion(f32[16,3,4,8,128]{4,3,2,1,0:T(8,128)} %get-tuple-element.5, pred[4,8,128]{2,1,0:T(8,128)(4,1)S(1)} %and_compare_fusion), kind=kLoop, calls=%fused_computation | loop fusion | flops 196608 | bytes 1576960 | tf_op jit(solution)/shard_map/jit(_where)/select_n | solution.py:660
  (2 shorter events, 0.0 us)

commit v3 on v2

--- a/solution.py
+++ b/solution.py
@@ -121,15 +121,23 @@
     lax.fori_loop(0, 48, place_start, 0, unroll=4)
     pl.semaphore_wait(barrier, len(friends))
 
-    def halo(n):
+    def halo(n, h):
+        part = pl.ds(24 * h, 24)
         return [
-            remote(yy.at[n, 4], yy.at[n, 0], y_send.at[n, 0], y_recv.at[n, 0], nxt),
-            remote(yy.at[n, 1], yy.at[n, 5], y_send.at[n, 1], y_recv.at[n, 1], prv),
+            remote(yy.at[n, 4, part], yy.at[n, 0, part], y_send.at[n, h, 0], y_recv.at[n, h, 0], nxt),
+            remote(yy.at[n, 1, part], yy.at[n, 5, part], y_send.at[n, h, 1], y_recv.at[n, h, 1], prv),
         ]
 
-    halos = halo(0)
-    for c in halos:
-        c.start()
+    def begin(copies):
+        for c in copies:
+            c.start()
+        return copies
+
+    def end(copies):
+        for c in copies:
+            c.wait()
+
+    halos = [begin(halo(0, h)) for h in range(2)]
 
     load_smear.wait()
 
@@ -168,10 +176,10 @@
             c.start()
             link_copies.append(c)
 
-    def local_pass(n):
+    def local_pass(n, h):
         def step(i, _):
-            x = i >> 2
-            base = (i & 3) * 12
+            x = i >> 1
+            base = 24 * h + (i & 1) * 12
             field = [[yy[n, 1 + x, base + v * 3 + c] for c in range(3)] for v in range(4)]
             acc = [[jnp.zeros((8, 128), F32)] * 3 for _ in range(4)]
             for d in range(4):
@@ -189,12 +197,12 @@
                     hh[x, base + v * 3 + c] = acc[v][c]
             return 0
 
-        lax.fori_loop(0, 16, step, 0)
-
-    def x_pass(n, plane_of, count, finish):
+        lax.fori_loop(0, 8, step, 0)
+
+    def x_pass(n, h, plane_of, count, finish):
         def step(i, _):
-            x = plane_of(i >> 2)
-            base = (i & 3) * 12
+            x = plane_of(i >> 1)
+            base = 24 * h + (i & 1) * 12
             for back in (False, True):
                 links = [sx[x if back else 1 + x, e] for e in range(9)]
                 for v in range(4):
@@ -210,7 +218,7 @@
                             finish(x, base + v * 3 + c, acc[c])
             return 0
 
-        lax.fori_loop(0, 4 * count, step, 0)
+        lax.fori_loop(0, 2 * count, step, 0)
 
     lflat = lraw.reshape(8 * 192, 128)
 
@@ -230,41 +238,38 @@
         return 0
 
     for n in range(3):
-        local_pass(n)
-        if n == 0:
-            sx_copy.wait()
-        if n == 2:
-            for c in own_links + link_copies:
-                c.wait()
-            lax.fori_loop(0, 8, place_links, 0)
-            link_halos = [
-                remote(tl.at[3, 0, 0], tx.at[0, 3], lh_send.at[0, 0], lh_recv.at[0, 0], nxt),
-                remote(tl.at[pl.ds(1, 3), 1, 0], tx.at[1, pl.ds(1, 3)], lh_send.at[0, 1], lh_recv.at[0, 1], nxt),
-                remote(tl.at[:, 0, 1, :, pl.ds(7, 1)], tyh.at[0, :, :, pl.ds(7, 1)],
-                       lh_send.at[1, 0], lh_recv.at[1, 0], ynxt),
-                remote(tl.at[:, 1, 1, :, pl.ds(5, 3)], tyh.at[1, :, :, pl.ds(5, 3)],
-                       lh_send.at[1, 1], lh_recv.at[1, 1], ynxt),
-            ]
-        for c in halos:
-            c.wait()
-
-        def finish(x, comp, acc, n=n):
-            if n == 0:
-                value = (-0.5 / HALF_WIDTH) * yy[0, 1 + x, comp] - (1.0 / HALF_WIDTH) * acc
-            else:
-                value = ((-1.0 / HALF_WIDTH) * yy[n, 1 + x, comp] - (2.0 / HALF_WIDTH) * acc
-                         - yy[n - 1, 1 + x, comp])
-            yy[n + 1, 1 + x, comp] = value
-
-        x_pass(n, lambda i: 3 * i, 2, finish)
-        if n < 2:
-            halos = halo(n + 1)
-            for c in halos:
-                c.start()
-        if n == 2:
-            for c in link_halos:
-                c.start()
-        x_pass(n, lambda i: 1 + i, 2, finish)
+        for h in range(2):
+            local_pass(n, h)
+            if n == 0 and h == 0:
+                sx_copy.wait()
+            if n == 2 and h == 0:
+                for c in own_links + link_copies:
+                    c.wait()
+                lax.fori_loop(0, 8, place_links, 0)
+                link_halos = [
+                    remote(tl.at[3, 0, 0], tx.at[0, 3], lh_send.at[0, 0], lh_recv.at[0, 0], nxt),
+                    remote(tl.at[pl.ds(1, 3), 1, 0], tx.at[1, pl.ds(1, 3)], lh_send.at[0, 1], lh_recv.at[0, 1], nxt),
+                    remote(tl.at[:, 0, 1, :, pl.ds(7, 1)], tyh.at[0, :, :, pl.ds(7, 1)],
+                           lh_send.at[1, 0], lh_recv.at[1, 0], ynxt),
+                    remote(tl.at[:, 1, 1, :, pl.ds(5, 3)], tyh.at[1, :, :, pl.ds(5, 3)],
+                           lh_send.at[1, 1], lh_recv.at[1, 1], ynxt),
+                ]
+            end(halos[h])
+
+            def finish(x, comp, acc, n=n):
+                if n == 0:
+                    value = (-0.5 / HALF_WIDTH) * yy[0, 1 + x, comp] - (1.0 / HALF_WIDTH) * acc
+                else:
+                    value = ((-1.0 / HALF_WIDTH) * yy[n, 1 + x, comp] - (2.0 / HALF_WIDTH) * acc
+                             - yy[n - 1, 1 + x, comp])
+                yy[n + 1, 1 + x, comp] = value
+
+            x_pass(n, h, lambda i: 3 * i, 2, finish)
+            if n < 2:
+                halos[h] = begin(halo(n + 1, h))
+            if n == 2 and h == 0:
+                begin(link_halos)
+            x_pass(n, h, lambda i: 1 + i, 2, finish)
 
     def products(left, right):
         def step(k, _):
@@ -336,9 +341,7 @@
     for c in g_chips:
         c.start()
 
-    halos = halo(3)
-    for c in halos:
-        c.start()
+    halos = [begin(halo(3, h)) for h in range(2)]
     for c in link_halos:
         c.wait()
 
@@ -428,6 +431,20 @@
     def entry(k, j):
         return jnp.broadcast_to(cb[pl.ds(16 * j + k, 1), :], (8, 128))
 
+    def d_halo(n, h):
+        part = pl.ds(12 * h, 12)
+        return [
+            remote(ee.at[n, pl.ds(4, 3), part], ee.at[n, pl.ds(0, 3), part],
+                   dx_send.at[n, h, 0], dx_recv.at[n, h, 0], nxt),
+            remote(ee.at[n, pl.ds(3, 3), part], ee.at[n, pl.ds(7, 3), part],
+                   dx_send.at[n, h, 1], dx_recv.at[n, h, 1], prv),
+            remote(ee.at[n, pl.ds(3, 4), part, pl.ds(5, 3)], hp.at[n, :, part, pl.ds(5, 3)],
+                   dy_send.at[n, h, 0], dy_recv.at[n, h, 0], ynxt),
+            remote(ee.at[n, pl.ds(3, 4), part, pl.ds(0, 3)], hn.at[n, :, part, pl.ds(0, 3)],
+                   dy_send.at[n, h, 1], dy_recv.at[n, h, 1], yprv),
+        ]
+
+    d_copies = [None, None]
     for pair in range(8):
         same = [jnp.where(high_half, entry(pair + 8, j + 8), entry(pair, j)) for j in range(pair + 1)]
         cross = [jnp.where(high_half, entry(pair + 8, j), 0.0) for j in range(8)]
@@ -444,21 +461,13 @@
             return total
 
         mom[0, pair] = lax.fori_loop(0, 4, mix, jnp.zeros((8, 128), F32))
-
-    def d_halo(n):
-        return [
-            remote(ee.at[n, pl.ds(4, 3)], ee.at[n, pl.ds(0, 3)], dx_send.at[n, 0], dx_recv.at[n, 0], nxt),
-            remote(ee.at[n, pl.ds(3, 3)], ee.at[n, pl.ds(7, 3)], dx_send.at[n, 1], dx_recv.at[n, 1], prv),
-            remote(ee.at[n, pl.ds(3, 4), :, pl.ds(5, 3)], hp.at[n, :, :, pl.ds(5, 3)],
-                   dy_send.at[n, 0], dy_recv.at[n, 0], ynxt),
-            remote(ee.at[n, pl.ds(3, 4), :, pl.ds(0, 3)], hn.at[n, :, :, pl.ds(0, 3)],
-                   dy_send.at[n, 1], dy_recv.at[n, 1], yprv),
-        ]
-
-    def inner_pass(n, pi):
+        if pair & 3 == 3:
+            d_copies[pair >> 2] = begin(d_halo(0, pair >> 2))
+
+    def inner_pass(n, h, pi):
         def step(i, _):
-            x = i >> 1
-            base = (i & 1) * 12
+            x = i
+            base = 12 * h
             rho = (x + pi) & 1
             field = [[ee[n, 3 + x, base + v * 3 + c] for c in range(3)] for v in range(4)]
             acc = [[jnp.zeros((8, 128), F32)] * 3 for _ in range(4)]
@@ -479,15 +488,15 @@
                     h2[x, base + v * 3 + c] = acc[v][c]
             return 0
 
-        lax.fori_loop(0, 8, step, 0)
-
-    def outer_pass(n, pi, store):
-        for pair in range(8):
-            mom[n + 1, pair] = jnp.zeros((8, 128), F32)
+        lax.fori_loop(0, 4, step, 0)
+
+    def outer_pass(n, h, pi, store):
+        for v in range(4):
+            mom[n + 1, 4 * h + v] = jnp.zeros((8, 128), F32)
 
         def step(i, _):
-            x = i >> 1
-            base = (i & 1) * 12
+            x = i
+            base = 12 * h
             acc = [[h2[x, base + v * 3 + c] for c in range(3)] for v in range(4)]
             for d in range(8):
                 links = [ll[pi, x, d, e] for e in range(9)]
@@ -507,11 +516,11 @@
                 for c in range(3):
                     if store:
                         ee[n + 1, 3 + x, base + v * 3 + c] = acc[v][c]
-                mom[n + 1, (i & 1) * 4 + v] += (
+                mom[n + 1, 4 * h + v] += (
                     acc[v][0] * acc[v][0] + acc[v][1] * acc[v][1] + acc[v][2] * acc[v][2])
             return 0
 
-        lax.fori_loop(0, 8, step, 0)
+        lax.fori_loop(0, 4, step, 0)
 
     def flat_to_square(tile):
         total = jnp.zeros((16, 128), F32)
@@ -523,19 +532,15 @@
 
     for n in range(3):
         pi = 1 - (n & 1)
-        d_copies = d_halo(n)
-        for c in d_copies:
-            c.start()
-        inner_pass(n, pi)
+        inner_pass(n, 0, pi)
         if n == 0:
-            local_pass(3)
-            for c in halos:
-                c.wait()
-
             def keep_image(x, comp, acc):
                 af[x, comp] = 6.0 * yy[3, 1 + x, comp] - acc
 
-            x_pass(3, lambda i: i, 4, keep_image)
+            for g in range(2):
+                local_pass(3, g)
+                end(halos[g])
+                x_pass(3, g, lambda i: i, 4, keep_image)
             kone[0] = products(lambda x, e: yy[3, 1 + x, e], lambda x, e: af[x, e])
             k_partner = to_partner(kone, 1)
             k_partner.start()
@@ -557,9 +562,13 @@
                                    precision=HIGH, preferred_element_type=F32)
             proj_ref[0] = lax.dot_general(half, weights, (((1,), (0,)), ((), ())),
                                           precision=HIGH, preferred_element_type=F32)
-        for c in d_copies:
-            c.wait()
-        outer_pass(n, pi, n < 2)
+        for h in range(2):
+            if h == 1:
+                inner_pass(n, 1, pi)
+            end(d_copies[h])
+            outer_pass(n, h, pi, n < 2)
+            if n < 2:
+                d_copies[h] = begin(d_halo(n + 1, h))
 
     prod[...] = jnp.zeros((256, 128), F32)
     for m in range(4):
@@ -646,9 +655,9 @@
             vm(2, 8, 128), vm(8, 8, 128), vm(8, 8, 128),
             vm(2, 8, 128), vm(8, 8, 128),
             vm(2, 8, 128), vm(8, 8, 128), vm(8, 8, 128),
-            dma(2), dma(4, 2), dma(4, 2), dma(), dma(), dma(2, 7), dma(2, 7), dma(2),
+            dma(2), dma(4, 2, 2), dma(4, 2, 2), dma(), dma(), dma(2, 7), dma(2, 7), dma(2),
             dma(2, 2), dma(2, 2), dma(7), dma(7), dma(),
-            dma(3, 2), dma(3, 2), dma(3, 2), dma(3, 2),
+            dma(3, 2, 2), dma(3, 2, 2), dma(3, 2, 2), dma(3, 2, 2),
             dma(3), dma(3), dma(3, 7), dma(3, 7), dma(2, 7), dma(2, 7),
         ],
         compiler_params=pltpu.CompilerParams(

time: 109 us -> 103 us (0.945)
  Pallas kernels: 104 us -> 98.8 us
    pallas_call x1, Pallas kernels: 104 us -> 98.8 us  [body(): pl.pallas_call(kernel, out_shape=(jax.ShapeDtypeStruct((1, 16, 16), F32),...]
where the time goes in v3:
time: 103 us
  Pallas kernels  98.8 us (96%)
  other arithmetic  3.4 us (3%)
    pallas_call x1, Pallas kernels, body(): pl.pallas_call(kernel, out_shape=(jax.ShapeDtypeStruct((1, 16, 16), F32),...  98.8 us
    select_n x1, other arithmetic, body(): return (projected * (1.0 / SITES), jnp.where(even, filled, 0.0))  2.08 us

profile of v3, /device:TPU:0, one launch (start us, length us, event | category | flops | bytes accessed | tf_op | source)
XLA Modules:
  0.0 102.9 jit_solution(7081160988063133686)
XLA Ops:
  0.7 98.8 %distill.1 = (f32[1,16,16]{2,1,0:T(8,128)}, f32[16,3,4,8,128]{4,3,2,1,0:T(8,128)}) custom-call(f32[1536,128]{1,0:T(8,128)} %bitcast.20, f32[864,128]{1,0:T(8,128)} %bitcast.23, f32[4,9,8,4,128]{4,3,2,1,0:T(4,128)} %bitcast.21, f32[4,9,8,4,128]{4,3,2,1,0:T(4,128)} %bitcast.22), custom_call_target="tpu_custom_call" | custom-call | tf_op jit(solution)/shard_map/distill/pallas_call | solution.py:641
  99.5 1.3 %broadcast_multiply_fusion = f32[1,16,16]{2,1,0:T(8,128)} fusion(f32[1,16,16]{2,1,0:T(8,128)} %get-tuple-element.4), kind=kLoop, calls=%fused_computation.2 | loop fusion | flops 256 | bytes 2048 | tf_op jit(solution)/shard_map/mul | solution.py:669
  100.8 2.1 %broadcast_select_fusion = f32[16,3,4,8,128]{4,3,2,1,0:T(8,128)} fusion(f32[16,3,4,8,128]{4,3,2,1,0:T(8,128)} %get-tuple-element.5, pred[4,8,128]{2,1,0:T(8,128)(4,1)S(1)} %and_compare_fusion), kind=kLoop, calls=%fused_computation | loop fusion | flops 196608 | bytes 1576960 | tf_op jit(solution)/shard_map/jit(_where)/select_n | solution.py:669
  (2 shorter events, 0.0 us)

commit v4 on v3

--- a/solution.py
+++ b/solution.py
@@ -70,12 +70,12 @@
     ix[EX + 1] = (chunk << 4) | 8 | (low >> 1)
 
 
-def kernel(start_ref, smear_ref, fat_ref, naik_ref, proj_ref, out_ref,
+def kernel(start_ref, smear_ref, fat_ref, naik_ref, proj_ref, source_ref, second_ref, weight_ref,
            raw, sraw, yy, sx, syz, hh, af, prod, fs, fr, lraw, tl, tx, tyh, ll,
-           ee, hn, hp, h2, fp, fps, ix, cb, mom, gone, gslot, gtm, kone, kslot, sone, sslot, stm,
+           ee, hn, hp, h2, fp, fps, ix, cb, mom, gone, gslot, gtm, sone, sslot, stm,
            in_sem, y_send, y_recv, sx_send, sx_recv, l_send, l_recv, l_own, lh_send, lh_recv,
            f_send, f_recv, f_own, dx_send, dx_recv, dy_send, dy_recv,
-           c_send, c_recv, r_send, r_recv, t_send, t_recv):
+           c_send, c_recv, r_send, r_recv, t_send, t_recv, out_sem):
     t = lax.axis_index("tm")
     s = lax.axis_index("space")
     core = s & 1
@@ -330,21 +330,17 @@
         remote(part(fs, (t + d) & 7), part(fr, t), f_send.at[d - 1], f_recv.at[d - 1], times[d - 1])
         for d in range(1, 8)
     ]
-    for c in f_copies:
-        c.start()
     f_local = pltpu.make_async_copy(part(fs, t), part(fr, t), f_own)
-    f_local.start()
 
     g_partner.wait()
     gslot[chip] = gone[0] + gone[1]
     g_chips = to_chips(gslot, 0)
     for c in g_chips:
         c.start()
+    for c in f_copies + [f_local]:
+        c.start()
 
     halos = [begin(halo(3, h)) for h in range(2)]
-    for c in link_halos:
-        c.wait()
-
     chunk = lane >> 4
 
     def fill_links(i, _):
@@ -382,7 +378,8 @@
                     ll[pi, x, (mu * 2 + kind) * 2 + 1, e] = down * bwd[mu]
         return 0
 
-    lax.fori_loop(0, 36, fill_links, 0)
+    end(link_halos)
+    lax.fori_loop(0, 12, fill_links, 0)
 
     for c in g_chips:
         c.wait()
@@ -390,6 +387,7 @@
     g_times = to_times(gtm, 0)
     for c in g_times:
         c.start()
+    lax.fori_loop(12, 36, fill_links, 0)
 
     for c in f_copies:
         c.wait()
@@ -541,27 +539,7 @@
                 local_pass(3, g)
                 end(halos[g])
                 x_pass(3, g, lambda i: i, 4, keep_image)
-            kone[0] = products(lambda x, e: yy[3, 1 + x, e], lambda x, e: af[x, e])
-            k_partner = to_partner(kone, 1)
-            k_partner.start()
-        if n == 1:
-            k_partner.wait()
-            kslot[chip] = kone[0] + kone[1]
-            k_chips = to_chips(kslot, 1)
-            for c in k_chips:
-                c.start()
-        if n == 2:
-            for c in k_chips:
-                c.wait()
-            square = flat_to_square(total_of(kslot))
-            pick = jnp.where(lane == t * 16, 1.0, 0.0).astype(F32)
-            weights = lax.dot_general(pick, cb[...], (((1,), (1,)), ((), ())),
-                                      precision=HIGH, preferred_element_type=F32)
-            weights = flat_to_square(jnp.where(row == 0, weights[:, :128], weights[:, 128:]))
-            half = lax.dot_general(weights, square, (((0,), (0,)), ((), ())),
-                                   precision=HIGH, preferred_element_type=F32)
-            proj_ref[0] = lax.dot_general(half, weights, (((1,), (0,)), ((), ())),
-                                          precision=HIGH, preferred_element_type=F32)
+            sone[0, 1] = products(lambda x, e: yy[3, 1 + x, e], lambda x, e: af[x, e])
         for h in range(2):
             if h == 1:
                 inner_pass(n, 1, pi)
@@ -570,26 +548,42 @@
             if n < 2:
                 d_copies[h] = begin(d_halo(n + 1, h))
 
+    saved = [pltpu.make_async_copy(ee.at[2 * i, pl.ds(3, 4)], ref, out_sem.at[i])
+             for i, ref in enumerate((source_ref, second_ref))]
+    for c in saved:
+        c.start()
+
     prod[...] = jnp.zeros((256, 128), F32)
     for m in range(4):
         for pair in range(8):
             prod[pl.ds(8 * m + pair, 1), :] = jnp.sum(mom[m, pair], axis=0, keepdims=True)
     select = jnp.where(((lane >> 3) & 1) == row, 1.0, 0.0).astype(F32)
-    sone[0] = lax.dot_general(select, prod[pl.ds(0, 128), :], (((1,), (1,)), ((), ())),
+    sone[0, 0] = lax.dot_general(select, prod[pl.ds(0, 128), :], (((1,), (1,)), ((), ())),
                               precision=HIGH, preferred_element_type=F32)
-    s_partner = to_partner(sone, 2)
+    s_partner = to_partner(sone, 1)
     s_partner.start()
     s_partner.wait()
     sslot[chip] = sone[0] + sone[1]
-    s_chips = to_chips(sslot, 2)
+    s_chips = to_chips(sslot, 1)
     for c in s_chips:
         c.start()
     for c in s_chips:
         c.wait()
-    stm[t] = total_of(sslot)
+    both = total_of(sslot)
+    stm[t] = both[0]
     s_times = to_times(stm, 1)
     for c in s_times:
         c.start()
+
+    square = flat_to_square(both[1])
+    pick = jnp.where(lane == t * 16, 1.0, 0.0).astype(F32)
+    weights = lax.dot_general(pick, cb[...], (((1,), (1,)), ((), ())),
+                              precision=HIGH, preferred_element_type=F32)
+    weights = flat_to_square(jnp.where(row == 0, weights[:, :128], weights[:, 128:]))
+    half = lax.dot_general(weights, square, (((0,), (0,)), ((), ())),
+                           precision=HIGH, preferred_element_type=F32)
+    proj_ref[0] = lax.dot_general(half, weights, (((1,), (0,)), ((), ())),
+                                  precision=HIGH, preferred_element_type=F32) * (1.0 / SITES)
     for c in s_times:
         c.wait()
     n0 = total_of(stm)
@@ -603,26 +597,56 @@
     a = alpha0 * ratio + beta
     energy = 0.25 * rr * (1.0 + beta) + a * a * n1 - 2.0 * a * alpha0 * n2 + alpha0 * alpha0 * n3
     alpha1 = rr / energy
-    first = alpha0 + alpha1 * a
-    second = alpha1 * alpha0
-
-    def spread(v, pair):
-        low = jnp.broadcast_to(v[0:1, pair:pair + 1], (8, 128))
-        high = jnp.broadcast_to(v[1:2, pair:pair + 1], (8, 128))
+    weight_ref[...] = jnp.where(row < 2, alpha1 * alpha0, pltpu.roll(alpha0 + alpha1 * a, 2, 0))
+    for c in saved:
+        c.wait()
+
+
+def assemble(proj_ref, source_ref, second_ref, weight_ref, done_ref, out_ref,
+             small, weights, pp, ww, full, in_sem, out_sem):
+    loads = [pltpu.make_async_copy(weight_ref, weights, in_sem.at[0]),
+             pltpu.make_async_copy(proj_ref, small, in_sem.at[1])]
+    parts = [pl.ds(6 * i, 6) for i in range(4)]
+    fields = [
+        [pltpu.make_async_copy(ref.at[:, part], buf.at[:, part], in_sem.at[2 + 2 * i + j])
+         for j, (ref, buf) in enumerate(((source_ref, pp), (second_ref, ww)))]
+        for i, part in enumerate(parts)
+    ]
+    for c in loads + sum(fields, []):
+        c.start()
+    row, lane = tile_iota()
+    high_half = (lane & 8) != 0
+    spots = [(lane & 112) | 8 * h | ((lane & 15) >> 1) for h in range(2)]
+    even = [((x + row + (lane >> 4) + lane) & 1) == 0 for x in range(2)]
+    for c in loads:
+        c.wait()
+    done = pltpu.make_async_copy(small, done_ref, out_sem.at[0])
+    done.start()
+    stores = [done]
+
+    def spread(first, pair):
+        low = jnp.broadcast_to(weights[first:first + 1, pair:pair + 1], (8, 128))
+        high = jnp.broadcast_to(weights[first + 1:first + 2, pair:pair + 1], (8, 128))
         return jnp.where(high_half, high, low)
 
-    for pair in range(8):
-        ca = spread(first, pair)
-        cd = spread(second, pair)
-
-        def finish_out(x, _, pair=pair, ca=ca, cd=cd):
-            for c in range(3):
-                value = ca * ee[0, 3 + x, pair * 3 + c] + cd * ee[2, 3 + x, pair * 3 + c]
-                out_ref[pair, c, x] = lanes(value, ix[EX])
-                out_ref[pair + 8, c, x] = lanes(value, ix[EX + 1])
-            return 0
-
-        lax.fori_loop(0, 4, finish_out, 0, unroll=True)
+    for i in range(4):
+        for c in fields[i]:
+            c.wait()
+        for pair in (2 * i, 2 * i + 1):
+            ca = spread(2, pair)
+            cd = spread(0, pair)
+            for x in range(4):
+                for c in range(3):
+                    value = ca * pp[x, pair * 3 + c] + cd * ww[x, pair * 3 + c]
+                    for h in range(2):
+                        full[pair + 8 * h, c, x] = jnp.where(even[x & 1], lanes(value, spots[h]), 0.0)
+        for h in range(2):
+            where = pl.ds(8 * h + 2 * i, 2)
+            copy = pltpu.make_async_copy(full.at[where], out_ref.at[where], out_sem.at[1 + 2 * i + h])
+            copy.start()
+            stores.append(copy)
+    for c in stores:
+        c.wait()
 
 
 def rows_first(array, lead):
@@ -638,12 +662,13 @@
     dma = lambda *shape: pltpu.SemaphoreType.DMA(shape) if shape else pltpu.SemaphoreType.DMA
     anywhere = pl.BlockSpec(memory_space=pl.ANY)
     local = pl.BlockSpec(memory_space=pltpu.VMEM)
-    projected, filled = pl.pallas_call(
+    packed = jax.ShapeDtypeStruct((4, 24, 8, 128), F32)
+    parts = pl.pallas_call(
         kernel,
-        out_shape=(jax.ShapeDtypeStruct((1, 16, 16), F32),
-                   jax.ShapeDtypeStruct((16, 3, 4, 8, 128), F32)),
+        out_shape=(jax.ShapeDtypeStruct((1, 16, 16), F32), packed, packed,
+                   jax.ShapeDtypeStruct((8, 128), F32)),
         in_specs=[anywhere] * 4,
-        out_specs=(local, local),
+        out_specs=(local, anywhere, anywhere, local),
         scratch_shapes=[
             vm(1536, 128), vm(864, 128), vm(4, 6, 48, 8, 128), vm(5, 9, 8, 128), vm(4, 4, 9, 8, 128),
             vm(4, 48, 8, 128), vm(4, 48, 8, 128), vm(256, 128), vm(768, 128), vm(768, 128),
@@ -653,20 +678,27 @@
             vm(4, 24, 8, 128), vm(4, 24, 8, 128), pltpu.VMEM((SLOTS, 8, 128), jnp.int32),
             vm(256, 128), vm(4, 8, 8, 128),
             vm(2, 8, 128), vm(8, 8, 128), vm(8, 8, 128),
-            vm(2, 8, 128), vm(8, 8, 128),
-            vm(2, 8, 128), vm(8, 8, 128), vm(8, 8, 128),
+            vm(2, 2, 8, 128), vm(8, 2, 8, 128), vm(8, 8, 128),
             dma(2), dma(4, 2, 2), dma(4, 2, 2), dma(), dma(), dma(2, 7), dma(2, 7), dma(2),
             dma(2, 2), dma(2, 2), dma(7), dma(7), dma(),
             dma(3, 2, 2), dma(3, 2, 2), dma(3, 2, 2), dma(3, 2, 2),
-            dma(3), dma(3), dma(3, 7), dma(3, 7), dma(2, 7), dma(2, 7),
+            dma(2), dma(2), dma(2, 7), dma(2, 7), dma(2, 7), dma(2, 7), dma(2),
         ],
         compiler_params=pltpu.CompilerParams(
             collective_id=0, has_side_effects=True, vmem_limit_bytes=60 * 2**20),
         name="distill",
     )(start, smear, fat, naik)
-    place = [lax.broadcasted_iota(jnp.int32, (4, 8, 128), d) for d in range(3)]
-    even = ((place[0] + place[1] + (place[2] >> 4) + place[2]) & 1) == 0
-    return projected * (1.0 / SITES), jnp.where(even, filled, 0.0)
+    return pl.pallas_call(
+        assemble,
+        out_shape=(jax.ShapeDtypeStruct((1, 16, 16), F32),
+                   jax.ShapeDtypeStruct((16, 3, 4, 8, 128), F32)),
+        in_specs=[anywhere] * 4,
+        out_specs=(anywhere, anywhere),
+        scratch_shapes=[vm(1, 16, 16), vm(8, 128), vm(4, 24, 8, 128), vm(4, 24, 8, 128),
+                        vm(16, 3, 4, 8, 128), dma(10), dma(9)],
+        compiler_params=pltpu.CompilerParams(vmem_limit_bytes=60 * 2**20),
+        name="assemble",
+    )(*parts)
 
 
 def solution(mesh):

time: 103 us -> 99.6 us (0.967)
  other arithmetic: 3.4 us -> 0 us
    pallas_call x1, Pallas kernels: 98.8 us -> 96 us  [body(): pl.pallas_call(kernel, out_shape=(jax.ShapeDtypeStruct((1, 16, 16), F32),...]
    pallas_call x0 -> x1, Pallas kernels: none -> 2.84 us  [body(): pl.pallas_call(assemble, out_shape=(jax.ShapeDtypeStruct((1, 16, 16), F32...]
    select_n x1 -> x0, other arithmetic: 2.08 us -> none  [body(): return (projected * (1.0 / SITES), jnp.where(even, filled, 0.0))]
    mul x1 -> x0, other arithmetic: 1.3 us -> none  [body(): return (projected * (1.0 / SITES), jnp.where(even, filled, 0.0))]
where the time goes in v4:
time: 99.6 us; the launch traced here: 99.5 us
  Pallas kernels  98.8 us (99%)
    pallas_call x1, Pallas kernels, body(): pl.pallas_call(kernel, out_shape=(jax.ShapeDtypeStruct((1, 16, 16), F32),...  96 us
    pallas_call x1, Pallas kernels, body(): pl.pallas_call(assemble, out_shape=(jax.ShapeDtypeStruct((1, 16, 16), F32...  2.84 us

profile of v4, /device:TPU:0, one launch (start us, length us, event | category | flops | bytes accessed | tf_op | source)
XLA Modules:
  0.0 99.5 jit_solution(14719875799126210716)
XLA Ops:
  0.6 96.0 %distill.1 = (f32[1,16,16]{2,1,0:T(8,128)}, f32[4,24,8,128]{3,2,1,0:T(8,128)}, f32[4,24,8,128]{3,2,1,0:T(8,128)}, f32[8,128]{1,0:T(8,128)}) custom-call(f32[1536,128]{1,0:T(8,128)} %bitcast.20, f32[864,128]{1,0:T(8,128)} %bitcast.23, f32[4,9,8,4,128]{4,3,2,1,0:T(4,128)} %bitcast.21, f32[4,9,8,4,128]{4,3,2,1,0:T(4,128)} %bitcast.22), custom_call_target="tpu_custom_call" | custom-call | tf_op jit(solution)/shard_map/distill/pallas_call | solution.py:666
  96.6 2.8 %assemble.1 = (f32[1,16,16]{2,1,0:T(8,128)}, f32[16,3,4,8,128]{4,3,2,1,0:T(8,128)}) custom-call(f32[1,16,16]{2,1,0:T(8,128)} %get-tuple-element.6.proj_ref, f32[4,24,8,128]{3,2,1,0:T(8,128)} %get-tuple-element.7.source_ref, f32[4,24,8,128]{3,2,1,0:T(8,128)} %get-tuple-element.8.second_ref, f32[8,128]{1,0:T(8,128)} %get-tuple-element.9.weight_ref), custom_call_target="tpu_custom_call" | custom-call | tf_op jit(solution)/shard_map/assemble/pallas_call | solution.py:691

commit v5 on v4

--- a/solution.py
+++ b/solution.py
@@ -173,7 +173,6 @@
         for i, ref in enumerate((fat_ref, naik_ref)):
             c = remote(ref.at[:, pl.ds(0, 6), dest], lraw.at[t, i],
                        l_send.at[i, d - 1], l_recv.at[i, d - 1], (dest, s))
-            c.start()
             link_copies.append(c)
 
     def local_pass(n, h):
@@ -267,6 +266,8 @@
             x_pass(n, h, lambda i: 3 * i, 2, finish)
             if n < 2:
                 halos[h] = begin(halo(n + 1, h))
+            if n == 0 and h == 0:
+                begin(link_copies)
             if n == 2 and h == 0:
                 begin(link_halos)
             x_pass(n, h, lambda i: 1 + i, 2, finish)
@@ -531,7 +532,7 @@
     for n in range(3):
         pi = 1 - (n & 1)
         inner_pass(n, 0, pi)
-        if n == 0:
+        if n == 1:
             def keep_image(x, comp, acc):
                 af[x, comp] = 6.0 * yy[3, 1 + x, comp] - acc
 
@@ -539,6 +540,7 @@
                 local_pass(3, g)
                 end(halos[g])
                 x_pass(3, g, lambda i: i, 4, keep_image)
+        if n == 1:
             sone[0, 1] = products(lambda x, e: yy[3, 1 + x, e], lambda x, e: af[x, e])
         for h in range(2):
             if h == 1:
@@ -606,7 +608,7 @@
              small, weights, pp, ww, full, in_sem, out_sem):
     loads = [pltpu.make_async_copy(weight_ref, weights, in_sem.at[0]),
              pltpu.make_async_copy(proj_ref, small, in_sem.at[1])]
-    parts = [pl.ds(6 * i, 6) for i in range(4)]
+    parts = [pl.ds(12 * i, 12) for i in range(2)]
     fields = [
         [pltpu.make_async_copy(ref.at[:, part], buf.at[:, part], in_sem.at[2 + 2 * i + j])
          for j, (ref, buf) in enumerate(((source_ref, pp), (second_ref, ww)))]
@@ -629,10 +631,10 @@
         high = jnp.broadcast_to(weights[first + 1:first + 2, pair:pair + 1], (8, 128))
         return jnp.where(high_half, high, low)
 
-    for i in range(4):
+    for i in range(2):
         for c in fields[i]:
             c.wait()
-        for pair in (2 * i, 2 * i + 1):
+        for pair in range(4 * i, 4 * i + 4):
             ca = spread(2, pair)
             cd = spread(0, pair)
             for x in range(4):
@@ -641,7 +643,7 @@
                     for h in range(2):
                         full[pair + 8 * h, c, x] = jnp.where(even[x & 1], lanes(value, spots[h]), 0.0)
         for h in range(2):
-            where = pl.ds(8 * h + 2 * i, 2)
+            where = pl.ds(8 * h + 4 * i, 4)
             copy = pltpu.make_async_copy(full.at[where], out_ref.at[where], out_sem.at[1 + 2 * i + h])
             copy.start()
             stores.append(copy)

time: 99.6 us -> 97.9 us (0.983)
  Pallas kernels: 98.8 us -> 97.1 us
    pallas_call x1, Pallas kernels: 96 us -> 94.5 us  [body(): pl.pallas_call(kernel, out_shape=(jax.ShapeDtypeStruct((1, 16, 16), F32),...]
where the time goes in v5:
time: 97.9 us; the launch traced here: 97.8 us
  Pallas kernels  97.1 us (99%)
    pallas_call x1, Pallas kernels, body(): pl.pallas_call(kernel, out_shape=(jax.ShapeDtypeStruct((1, 16, 16), F32),...  94.5 us
    pallas_call x1, Pallas kernels, body(): pl.pallas_call(assemble, out_shape=(jax.ShapeDtypeStruct((1, 16, 16), F32...  2.6 us

profile of v5, /device:TPU:0, one launch (start us, length us, event | category | flops | bytes accessed | tf_op | source)
XLA Modules:
  0.0 97.8 jit_solution(16209111126670673924)
XLA Ops:
  0.6 94.5 %distill.1 = (f32[1,16,16]{2,1,0:T(8,128)}, f32[4,24,8,128]{3,2,1,0:T(8,128)}, f32[4,24,8,128]{3,2,1,0:T(8,128)}, f32[8,128]{1,0:T(8,128)}) custom-call(f32[1536,128]{1,0:T(8,128)} %bitcast.20, f32[864,128]{1,0:T(8,128)} %bitcast.23, f32[4,9,8,4,128]{4,3,2,1,0:T(4,128)} %bitcast.21, f32[4,9,8,4,128]{4,3,2,1,0:T(4,128)} %bitcast.22), custom_call_target="tpu_custom_call" | custom-call | tf_op jit(solution)/shard_map/distill/pallas_call | solution.py:668
  95.2 2.6 %assemble.1 = (f32[1,16,16]{2,1,0:T(8,128)}, f32[16,3,4,8,128]{4,3,2,1,0:T(8,128)}) custom-call(f32[1,16,16]{2,1,0:T(8,128)} %get-tuple-element.6.proj_ref, f32[4,24,8,128]{3,2,1,0:T(8,128)} %get-tuple-element.7.source_ref, f32[4,24,8,128]{3,2,1,0:T(8,128)} %get-tuple-element.8.second_ref, f32[8,128]{1,0:T(8,128)} %get-tuple-element.9.weight_ref), custom_call_target="tpu_custom_call" | custom-call | tf_op jit(solution)/shard_map/assemble/pallas_call | solution.py:693
